TPU v7x, 256 devices: a whole 4x4x8 slice. The times are simulated.
256 devices in a mesh: elem: 32 (over z, x_hi, core), mode: 8 (over y, x_lo).
Axes of the slice: x: 4 (x_hi: 2, x_lo: 2; x = x_hi * 2 + x_lo), y: 4, z: 8, core: 2. Of those that a mesh axis runs over, the one named last changes fastest.
Arguments:
- velocity: float32 [1024, 1024, 128], P(None, ('elem', 'mode')), may hold values from -6 to 6
- previous: float32 [1024, 1024, 128], P('mode', 'elem'), may hold values from -6 to 6
- derivative: float32 [128, 128], replicated, may hold values from -0.5 to 0.5
- stiffness: float32 [128, 128], replicated, as said below
- coupling: float32 [4, 128, 128], replicated, may hold values from -0.25 to 0.25
- reaction: float32 [1024], P('elem'), may hold values from 0.5 to 4
- axial_weight: float32 [1024], P('elem'), may hold values from 0.5 to 4
- neighbours: int32 [1024, 4], P('elem'), may hold values from -1 to 1023, as said below
Outputs:
- solution: float32 [1024, 1024, 128], P('mode', 'elem')
Inputs may be any that keep to these rules, and one draw needn't show every extreme that they name: `stiffness`: symmetric with a positive diagonal. `neighbours`: elements lie on a grid of 8 rows, periodic along the rows, and 4 columns a group of 32 elements, groups in order along the columns with walls at both ends. A group's first 8 elements form its first column and its last 8 its last column; a neighbour in another group is in the next or previous group, among its first or last 8 elements.
All inputs are finite; a program needn't handle non-finite values.
Results may differ from a plain program's by a relative error of at most 0.0001.
Values sent between devices are 32-bit elements; how exact they have to be, the bound alone decides.
No kernel may reach another device: no remote copies, remote signals or barrier semaphores. Data moves between devices by JAX's collectives and lax.ppermute only.
A program may use at most 128 MiB of HBM per device.

v0:
```python
import functools
import math

import jax
import jax.numpy as jnp
import numpy as np
from jax import lax
from jax.experimental import pallas as pl
from jax.experimental.pallas import tpu as pltpu
from jax.sharding import PartitionSpec as P

dt_step = 0.5
first_weight = 0.7
second_weight = 1.1

chunks = 1


def split(x):
    high = x.astype(jnp.bfloat16)
    low = (x - high.astype(jnp.float32)).astype(jnp.bfloat16)
    return high, low


def pair(x):
    return jnp.concatenate(split(x), axis=1)


def pair_weight(w):
    high, low = split(w)
    return jnp.concatenate(
        [jnp.concatenate([high, high], axis=1), jnp.concatenate([low, low], axis=1)], axis=0
    )


def dot_nt(x, w):
    return lax.dot_general(x, w, (((1,), (1,)), ((), ())), preferred_element_type=jnp.float32)


def times(x, w):
    y = dot_nt(x, w)
    n = y.shape[1] // 2
    return y[:, :n] + y[:, n:]


@functools.cache
def dft_tables(planes):
    half, quarter = planes // 2, planes // 4
    rows = np.arange(planes)
    waves = np.where(rows <= half, rows, rows - half)

    def table(picked, count):
        z = np.arange(count)
        phase = (waves[picked][:, None] * z[None, :]) % planes
        angle = 2.0 * np.pi / planes * phase
        t = np.where((picked <= half)[:, None], np.cos(angle), -np.sin(angle)) * planes**-0.5
        high = t.astype(np.float32).astype(jnp.bfloat16)
        low = (t - high.astype(np.float64)).astype(np.float32).astype(jnp.bfloat16)
        return np.concatenate([high, low], axis=1)

    odd = table(rows[1::2], half)
    even = np.concatenate([table(rows[2::4], quarter), table(rows[0::4], quarter)], axis=0)
    return odd, even


def dft3(t, h, l):
    k = t.shape[1] // 2
    dot = functools.partial(jnp.dot, preferred_element_type=jnp.float32)
    return dot(t[:, :k], h) + dot(t[:, :k], l) + dot(t[:, k:], h)


def pack_kernel(prev, tail, head, sems):
    rim = head.shape[1]
    elems = prev.shape[1]
    copies = [
        pltpu.make_async_copy(prev.at[:, pl.ds(elems - rim, rim), :], tail, sems.at[0]),
        pltpu.make_async_copy(prev.at[:, pl.ds(0, rim), :], head, sems.at[1]),
    ]
    for c in copies:
        c.start()
    for c in copies:
        c.wait()


def spectrum_kernel(tile, tail, head, vel_hbm, der, odd_hbm, even_hbm, *refs):
    outs, (vel, odd_table, even_table, dh, dl, eh, el, stage, sems, table_sems, out_sems) = refs[:chunks], refs[chunks:]
    nodes = der.shape[0]
    local = dh.shape[1] // nodes
    planes = vel.shape[0] // local
    quarter = planes // 4
    tiles = quarter // tile
    devices = outs[0].shape[0]
    reads = []
    for t in range(tiles):
        here = []
        for j in range(4):
            rows = pl.ds((j * quarter + t * tile) * local, tile * local)
            here.append(pltpu.make_async_copy(vel_hbm.at[rows, :], vel.at[rows, :], sems.at[t, j]))
            here[-1].start()
        reads.append(here)
    table_reads = [
        pltpu.make_async_copy(odd_hbm, odd_table, table_sems.at[0]),
        pltpu.make_async_copy(even_hbm, even_table, table_sems.at[1]),
    ]
    for c in table_reads:
        c.start()
    weight = pair_weight(der[...])

    for t in range(tiles):
        for c in reads[t]:
            c.wait()
        for e in range(local):
            cols = slice(e * nodes, (e + 1) * nodes)
            v = jnp.concatenate(
                [
                    vel[pl.ds((j * quarter + t * tile) * local + e, tile, stride=local), :]
                    for j in range(4)
                ],
                axis=0,
            )
            p = v - dt_step * v * times(pair(v), weight)
            p0, p1, p2, p3 = (p[j * tile : (j + 1) * tile] for j in range(4))
            s0, s1 = p0 + p2, p1 + p3
            here, there = slice(t * tile, (t + 1) * tile), slice(quarter + t * tile, quarter + (t + 1) * tile)
            dh[here, cols], dl[here, cols] = split(p0 - p2)
            dh[there, cols], dl[there, cols] = split(p1 - p3)
            eh[here, cols], el[here, cols] = split(s0 - s1)
            eh[there, cols], el[there, cols] = split(s0 + s1)

    for c in table_reads:
        c.wait()
    rows = stage.shape[3]
    group = 2
    writes = []
    for g in range(0, local, group):
        cols = slice(g * nodes, (g + group) * nodes)
        odd = dft3(odd_table[...], dh[:, cols], dl[:, cols])
        two = dft3(even_table[:quarter], eh[:quarter, cols], el[:quarter, cols])
        zero = dft3(even_table[quarter:], eh[quarter:, cols], el[quarter:, cols])
        for values, offset, stride in ((odd, 1, 2), (two, 2, 4), (zero, 0, 4)):
            n = rows // stride
            for m in range(devices):
                for c in range(chunks):
                    at = (m * chunks + c) * n
                    for e in range(group):
                        stage[c, m, g + e, pl.ds(offset, n, stride=stride), :] = values[
                            at : at + n, e * nodes : (e + 1) * nodes
                        ]
        for c in range(chunks):
            writes.append(
                pltpu.make_async_copy(
                    stage.at[c, :, pl.ds(g, group)], outs[c].at[:, pl.ds(g, group)], out_sems.at[c, g // group]
                )
            )
            writes[-1].start()
    for c in writes:
        c.wait()


def row_shift(first_row, count, planes, lanes):
    rows = first_row + lax.broadcasted_iota(jnp.int32, (count, lanes), 0)
    half = planes // 2
    waves = jnp.where(rows <= half, rows, rows - half).astype(jnp.float32)
    return 4.0 * (waves * (1.0 / half)) ** 2


def diagonal(stiff):
    n = stiff.shape[0]
    eye = lax.broadcasted_iota(jnp.int32, (n, n), 0) == lax.broadcasted_iota(jnp.int32, (n, n), 1)
    return jnp.sum(jnp.where(eye, stiff, 0.0), axis=0, keepdims=True)


def start_kernel(planes, chunk, meta, near, reaction, axial, prev, left, right, stiff, coupling, out, h, y, y0, y1):
    elems, rows, nodes = out.shape
    rim = left.shape[1] // 1
    group = meta[0] * elems
    prev = prev.reshape(rows * elems, nodes)
    left = left.reshape(rows * rim, nodes)
    right = right.reshape(rows * rim, nodes)

    for e in range(rim):
        h[e] = pair(left[pl.ds(e, rows, stride=rim), :])
        h[rim + elems + e] = pair(right[pl.ds(e, rows, stride=rim), :])
    for e in range(elems):
        v = prev[pl.ds(e, rows, stride=elems), :]
        out[e] = v
        h[rim + e] = pair(v)
    step = 8

    def fill(dst, w, a, b):
        for i in range(a, b, step):
            x = h[i : i + step].reshape(step * rows, 2 * nodes)
            dst[i - a : i - a + step] = times(x, w).reshape(step, rows, nodes)

    fill(y0, pair_weight(coupling[0]), 0, rim + elems)
    fill(y1, pair_weight(coupling[1]), rim, rim + elems + rim)
    y0[rim + elems] = jnp.zeros((rows, nodes), jnp.float32)
    y1[rim + elems] = jnp.zeros((rows, nodes), jnp.float32)
    for f in (2, 3):
        fill(y.at[f - 2], pair_weight(coupling[f]), rim, rim + elems)
        y[f - 2, elems] = jnp.zeros((rows, nodes), jnp.float32)
    fill(y.at[2], pair_weight(stiff[...]), rim, rim + elems)

    shift = row_shift(meta[1] * (chunks * rows) + chunk * rows, rows, planes, nodes)
    diag = diagonal(stiff[...])

    def place(e, f, low, high):
        n = near[e, f]
        return jnp.where(n >= 0, jnp.clip(n - group + low, 0, high - 1), high)

    def combine(e, carry):
        v = out[e]
        scaling = reaction[e] + shift * axial[e]
        total = y[2, e] + scaling * v
        total += y0[place(e, 0, rim, rim + elems)] + y1[place(e, 1, 0, rim + elems)]
        total += y[0, place(e, 2, 0, elems)] + y[1, place(e, 3, 0, elems)]
        out[e] = v - first_weight * total / (diag + scaling)
        return carry

    lax.fori_loop(0, elems, combine, 0)


def first_kernel(planes, chunk, meta, reaction, axial, base, rhs, stiff, out, head, tail):
    elems, rows, nodes = base.shape
    rim = head.shape[0]
    shift = row_shift(meta[1] * (chunks * rows) + chunk * rows, rows, planes, nodes)
    diag = diagonal(stiff[...])
    for e in range(elems):
        scaling = reaction[e] + shift * axial[e]
        v = base[e] + first_weight * rhs[e] / (diag + scaling)
        out[e] = v
        if e < rim:
            head[e] = v
        if e >= elems - rim:
            tail[e - (elems - rim)] = v


def second_kernel(planes, chunk, meta, near, reaction, axial, first, rhs, stiff, coupling, *refs):
    out, rest, h, y, stage, sem = refs[-6:]
    elems, rows, nodes = first.shape
    rim = rest.shape[0] // 2
    inner = elems - 2 * rim
    group = meta[0] * elems
    for e in range(elems):
        h[e] = pair(first[e])
    step = 8

    def fill(f, w):
        for i in range(0, elems, step):
            y[f, i : i + step] = times(h[i : i + step].reshape(step * rows, 2 * nodes), w).reshape(step, rows, nodes)

    for f in range(4):
        fill(f, pair_weight(coupling[f]))
        y[f, elems] = jnp.zeros((rows, nodes), jnp.float32)
    fill(4, pair_weight(stiff[...]))
    shift = row_shift(meta[1] * (chunks * rows) + chunk * rows, rows, planes, nodes)
    diag = diagonal(stiff[...])

    def place(e, f):
        at = near[e, f] - group
        return jnp.where((at >= 0) & (at < elems), at, elems)

    def combine(e):
        v = first[e]
        scaling = reaction[e] + shift * axial[e]
        total = y[4, e] + scaling * v
        for f in range(4):
            total += y[f, place(e, f)]
        return v + second_weight * (rhs[e] - total) / (diag + scaling)

    flat = stage.reshape(rows * inner, nodes)
    for e in range(rim, elems - rim):
        flat[pl.ds(e - rim, rows, stride=inner), :] = combine(e)
    copy = pltpu.make_async_copy(stage, out.at[pl.ds(chunk * rows, rows), pl.ds(rim, inner), :], sem)
    copy.start()
    for e in range(rim):
        rest[e] = combine(e)
        rest[rim + e] = combine(elems - rim + e)
    copy.wait()


def finish_kernel(planes, chunk, meta, near, reaction, axial, rest, left, right, stiff, coupling, kept, out, h, y, stage, sems):
    elems = near.shape[0]
    rim, rows, nodes = left.shape
    group = meta[0] * elems
    for e in range(rim):
        h[e] = pair(left[e])
        h[rim + e] = pair(right[e])
    shift = row_shift(meta[1] * (chunks * rows) + chunk * rows, rows, planes, nodes)
    diag = diagonal(stiff[...])
    copies = []
    for f in range(2):
        y[f, :rim] = times(
            h[f * rim : (f + 1) * rim].reshape(rim * rows, 2 * nodes), pair_weight(coupling[f])
        ).reshape(rim, rows, nodes)
        y[f, rim] = jnp.zeros((rows, nodes), jnp.float32)
        first_elem = f * (elems - rim)
        flat = stage.at[f].reshape(rows * rim, nodes)
        for i in range(rim):
            e = first_elem + i
            n = near[e, f]
            at = n - group + rim if f == 0 else n - group - elems
            at = jnp.where((n >= 0) & (at >= 0) & (at < rim), at, rim)
            scaling = reaction[e] + shift * axial[e]
            values = rest[f * rim + i] - second_weight * y[f, at] / (diag + scaling)
            flat[pl.ds(i, rows, stride=rim), :] = values
        copies.append(
            pltpu.make_async_copy(stage.at[f], out.at[pl.ds(chunk * rows, rows), pl.ds(first_elem, rim), :], sems.at[f])
        )
        copies[-1].start()
    for c in copies:
        c.wait()


vmem = pl.BlockSpec(memory_space=pltpu.VMEM)
smem = pl.BlockSpec(memory_space=pltpu.SMEM)
hbm = pl.BlockSpec(memory_space=pltpu.HBM)
anywhere = pl.BlockSpec(memory_space=pl.ANY)


def call(kernel, name, outs, out_specs, in_specs, scratch, args, mib, us, aliases=None):
    return pl.pallas_call(
        kernel,
        out_shape=outs,
        in_specs=in_specs,
        out_specs=out_specs,
        scratch_shapes=scratch,
        compiler_params=pltpu.CompilerParams(vmem_limit_bytes=mib * 2**20),
        cost_estimate=pl.CostEstimate(flops=int(us * 1e9), bytes_accessed=int(us * 3e6), transcendentals=0),
        input_output_aliases=aliases or {},
        name=name,
    )(*args)


def body(velocity, previous, derivative, stiffness, coupling, reaction, axial_weight, neighbours):
    planes, local, nodes = velocity.shape
    own_rows, elems, _ = previous.shape
    rim = elems // 4
    rows = own_rows // chunks
    devices = planes // own_rows
    groups = lax.axis_size("elem")
    f32, bf16 = jnp.float32, jnp.bfloat16
    struct = jax.ShapeDtypeStruct
    vm, dma = pltpu.VMEM, pltpu.SemaphoreType.DMA
    meta = jnp.stack([lax.axis_index("elem"), lax.axis_index("mode")]).astype(jnp.int32)
    to_right = [(i, i + 1) for i in range(groups - 1)]
    to_left = [(i + 1, i) for i in range(groups - 1)]

    side = struct((own_rows, rim, nodes), f32)
    tail, head = call(
        pack_kernel, "pack", (side, side), (vmem, vmem), [hbm], [dma((2,))], (previous,), 60, 1
    )
    prev_left = lax.ppermute(tail, "elem", to_right)
    prev_right = lax.ppermute(head, "elem", to_left)

    odd_table, even_table = dft_tables(planes)
    half, tile = planes // 2, 64
    spectrum = call(
        functools.partial(spectrum_kernel, tile),
        "spectrum",
        (struct((devices, local, rows, nodes), f32),) * chunks,
        (hbm,) * chunks,
        [anywhere, anywhere, hbm, vmem, hbm, hbm],
        [
            vm((planes * local, nodes), f32),
            vm(odd_table.shape, bf16),
            vm(even_table.shape, bf16),
            *([vm((half, local * nodes), bf16)] * 4),
            vm((chunks, devices, local, rows, nodes), f32),
            dma((planes // 4 // tile, 4)),
            dma((2,)),
            dma((chunks, local // 2)),
        ],
        (
            tail, head, velocity.reshape(planes * local, nodes), derivative,
            jnp.asarray(odd_table), jnp.asarray(even_table),
        ),
        60,
        40,
    )
    sent = [lax.all_to_all(s, "mode", split_axis=0, concat_axis=0, tiled=True) for s in spectrum]
    rhs = [s.reshape(elems, rows, nodes) for s in sent]

    field = struct((elems, rows, nodes), f32)
    scalars = (meta, neighbours, reaction, axial_weight)
    base = []
    for c in range(chunks):
        cut = slice(c * rows, (c + 1) * rows)
        base.append(
            call(
                functools.partial(start_kernel, planes, c),
                "start",
                field,
                vmem,
                [smem] * 4 + [vmem] * 5,
                [
                    vm((elems + 2 * rim, rows, 2 * nodes), bf16),
                    vm((3, elems + 1, rows, nodes), f32),
                    vm((elems + rim + 1, rows, nodes), f32),
                    vm((elems + rim + 1, rows, nodes), f32),
                ],
                (*scalars, previous[cut], prev_left[cut], prev_right[cut], stiffness, coupling),
                24,
                80,
            )
        )
    out = None
    tails = []
    for c in range(chunks):
        edge = struct((rim, rows, nodes), f32)
        first, head, tail = call(
            functools.partial(first_kernel, planes, c),
            "first",
            (field, edge, edge),
            (vmem,) * 3,
            [smem] * 3 + [vmem] * 3,
            [],
            (meta, reaction, axial_weight, base[c], rhs[c], stiffness),
            4,
            1,
        )
        left = lax.ppermute(tail, "elem", to_right)
        right = lax.ppermute(head, "elem", to_left)
        args = (*scalars, first, rhs[c], stiffness, coupling)
        whole = struct((own_rows, elems, nodes), f32)
        out, rest = call(
            functools.partial(second_kernel, planes, c),
            "second",
            (whole, struct((2 * rim, rows, nodes), f32)),
            (hbm, vmem),
            [smem] * 4 + [vmem] * 4 + [hbm] * (out is not None),
            [
                vm((elems, rows, 2 * nodes), bf16),
                vm((5, elems + 1, rows, nodes), f32),
                vm((rows, elems - 2 * rim, nodes), f32),
                dma,
            ],
            args if out is None else (*args, out),
            24,
            20,
            None if out is None else {len(args): 0},
        )
        tails.append((rest, left, right))
    for c, (rest, left, right) in enumerate(tails):
        args = (*scalars, rest, left, right, stiffness, coupling, out)
        out = call(
            functools.partial(finish_kernel, planes, c),
            "finish",
            whole,
            hbm,
            [smem] * 4 + [vmem] * 5 + [hbm],
            [
                vm((2 * rim, rows, 2 * nodes), bf16),
                vm((2, rim + 1, rows, nodes), f32),
                vm((2, rows, rim, nodes), f32),
                dma((2,)),
            ],
            args,
            8,
            1,
            {len(args) - 1: 0},
        )
    return out


def solution(mesh):
    return jax.shard_map(
        body,
        mesh=mesh,
        in_specs=(
            P(None, ("elem", "mode"), None),
            P("mode", "elem", None),
            P(),
            P(),
            P(),
            P("elem"),
            P("elem"),
            P("elem", None),
        ),
        out_specs=P("mode", "elem", None),
        check_vma=False,
    )
```

profile of v0, /device:TPU:97, one launch (start us, length us, event | category | flops | bytes accessed | tf_op | source)
XLA Modules:
  0.0 71.7 jit_solution(15149563373082847603)
XLA Ops:
  0.0 2.2 %pack.1 = (f32[128,8,128]{2,1,0:T(8,128)}, f32[128,8,128]{2,1,0:T(8,128)}) custom-call(f32[128,32,128]{2,1,0:T(8,128)} %prev.3), custom_call_target="tpu_custom_call" | custom-call | flops 1000000000 | bytes 3000000 | tf_op jit(solution)/shard_map/pack/pallas_call | solution.py:322
  2.2 5.2 %collective-permute-start = (f32[128,8,128]{2,1,0:T(8,128)}, f32[128,8,128]{2,1,0:T(8,128)S(1)}, u32[]{:S(2)}, u32[]{:S(2)}) collective-permute-start(f32[128,8,128]{2,1,0:T(8,128)} %get-tuple-element.12.tail), channel_id=1, source_target_pairs={{0,8},{8,16},{16,24},{24,32},{32,40},{40,48},{48,56},{56,64},{64,7... | collective-permute-start | bytes 1572872 | tf_op jit(solution)/shard_map/ppermute | solution.py:353
  7.4 1.9 %collective-permute-start.1 = (f32[128,8,128]{2,1,0:T(8,128)}, f32[128,8,128]{2,1,0:T(8,128)S(1)}, u32[]{:S(2)}, u32[]{:S(2)}) collective-permute-start(f32[128,8,128]{2,1,0:T(8,128)} %get-tuple-element.13.head), channel_id=1, source_target_pairs={{8,0},{16,8},{24,16},{32,24},{40,32},{48,40},{56,48},{64,56},{72,6... | collective-permute-start | bytes 1572872 | tf_op jit(solution)/shard_map/ppermute | solution.py:354
  9.4 6.2 %spectrum.1 = f32[8,4,128,128]{3,2,1,0:T(8,128)} custom-call(f32[128,8,128]{2,1,0:T(8,128)} %get-tuple-element.12.tail, f32[128,8,128]{2,1,0:T(8,128)} %get-tuple-element.13.head, f32[4096,128]{1,0:T(8,128)} %bitcast.6, f32[128,128]{1,0:T(8,128)} %der.1, bf16[512,1024]{1,0:T(8,128)(2,1)} %constant.13.clone.odd_hbm, bf16[512,512]{1,0:T(8,128)(2,1)} %constant.14.clone.even_hbm), custom_call_target="tpu_custom_call" | custom-call | flops 40000000000 | bytes 120000000 | tf_op jit(solution)/shard_map/spectrum/pallas_call | solution.py:322
  15.6 0.0 copy-start.7
  15.6 0.0 copy-start.2
  15.6 0.0 copy-start.4
  15.6 0.0 copy-start.5
  15.6 4.4 %all-to-all-start = ((f32[8,4,128,128]{3,2,1,0:T(8,128)}), f32[8,4,128,128]{3,2,1,0:T(8,128)S(1)}, u32[]{:S(2)}, u32[]{:S(2)}) async-start(f32[8,4,128,128]{3,2,1,0:T(8,128)} %spectrum.1), calls=%async_computation | async-start | bytes 4194304 | tf_op jit(solution)/shard_map/all_to_all | solution.py:381
  20.0 0.1 copy.14.near
  20.1 0.1 pad_add_fusion.meta
  20.2 0.8 %collective-permute-done.1.right = f32[128,8,128]{2,1,0:T(8,128)S(1)} collective-permute-done((f32[128,8,128]{2,1,0:T(8,128)}, f32[128,8,128]{2,1,0:T(8,128)S(1)}, u32[]{:S(2)}, u32[]{:S(2)}) %collective-permute-start.1) | collective-permute-done | bytes 524320 | tf_op jit(solution)/shard_map/ppermute | solution.py:354
  21.0 0.0 copy-start.6
  21.0 1.6 %copy-done.6 = f32[128,32,128]{2,1,0:T(8,128)S(1)} copy-done((f32[128,32,128]{2,1,0:T(8,128)S(1)}, f32[128,32,128]{2,1,0:T(8,128)}, u32[]{:S(2)}) %copy-start.6) | copy-done | bytes 2097176
  22.6 6.4 %start.1.base = f32[32,128,128]{2,1,0:T(8,128)S(1)} custom-call(s32[2]{0:T(128)S(1)} %pad_add_fusion.meta, s32[32,4]{1,0:T(8,128)S(1)} %copy.14.near, f32[32]{0:T(128)S(1)} %copy-done.4, f32[32]{0:T(128)S(1)} %copy-done.5, f32[128,32,128]{2,1,0:T(8,128)S(1)} %copy-done.6, f32[128,8,128]{2,1,0:T(8,128)S(1)} %collective-permute-done.left, ...), custom_call_target="tpu_custom_call" | custom-call | flops 80000000000 | bytes 240000000 | tf_op jit(solution)/shard_map/start/pallas_call | solution.py:322
  28.9 1.3 %copy-done = f32[32,128,128]{2,1,0:T(8,128)} copy-done((f32[32,128,128]{2,1,0:T(8,128)}, f32[32,128,128]{2,1,0:T(8,128)S(1)}, u32[]{:S(2)}) %copy-start) | copy-done | bytes 2097176
  30.2 15.1 %all-to-all-done = f32[8,4,128,128]{3,2,1,0:T(8,128)S(1)} async-done(((f32[8,4,128,128]{3,2,1,0:T(8,128)}), f32[8,4,128,128]{3,2,1,0:T(8,128)S(1)}, u32[]{:S(2)}, u32[]{:S(2)}) %all-to-all-start) | async-done | bytes 2097184 | tf_op jit(solution)/shard_map/all_to_all | solution.py:381
  45.4 1.6 %copy-done.1 = f32[32,128,128]{2,1,0:T(8,128)S(1)} copy-done((f32[32,128,128]{2,1,0:T(8,128)S(1)}, f32[32,128,128]{2,1,0:T(8,128)}, u32[]{:S(2)}) %copy-start.1) | copy-done | bytes 2097176
  47.0 1.1 %first.1 = (f32[32,128,128]{2,1,0:T(8,128)S(1)}, f32[8,128,128]{2,1,0:T(8,128)S(1)}, f32[8,128,128]{2,1,0:T(8,128)S(1)}) custom-call(s32[2]{0:T(128)S(1)} %pad_add_fusion.meta, f32[32]{0:T(128)S(1)} %copy-done.4, f32[32]{0:T(128)S(1)} %copy-done.5, f32[32,128,128]{2,1,0:T(8,128)S(1)} %copy-done.1, f32[32,128,128]{2,1,0:T(8,128)S(1)} %bitcast.4, ...), custom_call_target="tpu_custom_call" | custom-call | flops 1000000000 | bytes 3000000 | tf_op jit(solution)/shard_map/first/pallas_call | solution.py:322
  48.1 8.7 %collective-permute-start.2 = (f32[8,128,128]{2,1,0:T(8,128)S(1)}, f32[8,128,128]{2,1,0:T(8,128)S(1)}, u32[]{:S(2)}, u32[]{:S(2)}) collective-permute-start(f32[8,128,128]{2,1,0:T(8,128)S(1)} %get-tuple-element.16), channel_id=1, source_target_pairs={{0,8},{8,16},{16,24},{24,32},{32,40},{40,48},{48,56},{56,64},{64,7... | collective-permute-start | bytes 1572872 | tf_op jit(solution)/shard_map/ppermute | solution.py:422
  56.7 2.1 %collective-permute-start.3 = (f32[8,128,128]{2,1,0:T(8,128)S(1)}, f32[8,128,128]{2,1,0:T(8,128)S(1)}, u32[]{:S(2)}, u32[]{:S(2)}) collective-permute-start(f32[8,128,128]{2,1,0:T(8,128)S(1)} %get-tuple-element.17), channel_id=1, source_target_pairs={{8,0},{16,8},{24,16},{32,24},{40,32},{48,40},{56,48},{64,56},{72,6... | collective-permute-start | bytes 1572872 | tf_op jit(solution)/shard_map/ppermute | solution.py:423
  58.9 5.8 %second.1 = (f32[128,32,128]{2,1,0:T(8,128)}, f32[16,128,128]{2,1,0:T(8,128)S(1)}) custom-call(s32[2]{0:T(128)S(1)} %pad_add_fusion.meta, s32[32,4]{1,0:T(8,128)S(1)} %copy.14.near, f32[32]{0:T(128)S(1)} %copy-done.4, f32[32]{0:T(128)S(1)} %copy-done.5, f32[32,128,128]{2,1,0:T(8,128)S(1)} %get-tuple-element.14.first, f32[32,128,128]{2,1,0:T(8,128)S(1)} %bitcast.5, ...), custom_call_target="tpu_custom_call" | custom-call | flops 20000000000 | bytes 60000000 | tf_op jit(solution)/shard_map/second/pallas_call | solution.py:322
  64.6 4.4 %collective-permute-done.3.right = f32[8,128,128]{2,1,0:T(8,128)S(1)} collective-permute-done((f32[8,128,128]{2,1,0:T(8,128)S(1)}, f32[8,128,128]{2,1,0:T(8,128)S(1)}, u32[]{:S(2)}, u32[]{:S(2)}) %collective-permute-start.3) | collective-permute-done | bytes 524320 | tf_op jit(solution)/shard_map/ppermute | solution.py:423
  69.0 2.6 %finish.1 = f32[128,32,128]{2,1,0:T(8,128)} custom-call(s32[2]{0:T(128)S(1)} %pad_add_fusion.meta, s32[32,4]{1,0:T(8,128)S(1)} %copy.14.near, f32[32]{0:T(128)S(1)} %copy-done.4, f32[32]{0:T(128)S(1)} %copy-done.5, f32[16,128,128]{2,1,0:T(8,128)S(1)} %get-tuple-element.15.rest, ...), custom_call_target="tpu_custom_call", output_to_operand_aliasing={{}: (9, {})} | custom-call | flops 1000000000 | bytes 3000000 | tf_op jit(solution)/shard_map/finish/pallas_call | solution.py:322
  (10 shorter events, 0.0 us)
Async XLA Ops:
  2.2 18.0 %collective-permute-start = (f32[128,8,128]{2,1,0:T(8,128)}, f32[128,8,128]{2,1,0:T(8,128)S(1)}, u32[]{:S(2)}, u32[]{:S(2)}) collective-permute-start(f32[128,8,128]{2,1,0:T(8,128)} %get-tuple-element.12.tail), channel_id=1, source_target_pairs={{0,8},{8,16},{16,24},{24,32},{32,40},{40,48},{48,56},{56,64},{64,7... | collective-permute-start | bytes 1572872 | tf_op jit(solution)/shard_map/ppermute | solution.py:353
  7.4 13.5 %collective-permute-start.1 = (f32[128,8,128]{2,1,0:T(8,128)}, f32[128,8,128]{2,1,0:T(8,128)S(1)}, u32[]{:S(2)}, u32[]{:S(2)}) collective-permute-start(f32[128,8,128]{2,1,0:T(8,128)} %get-tuple-element.13.head), channel_id=1, source_target_pairs={{8,0},{16,8},{24,16},{32,24},{40,32},{48,40},{56,48},{64,56},{72,6... | collective-permute-start | bytes 1572872 | tf_op jit(solution)/shard_map/ppermute | solution.py:354
  15.6 4.4 %copy-start.7 = (s32[32,4]{0,1:T(4,128)S(1)}, s32[32,4]{0,1:T(4,128)}, u32[]{:S(2)}) copy-start(s32[32,4]{0,1:T(4,128)} %param.17) | copy-start | bytes 1540
  15.6 5.3 %copy-start.2 = (f32[128,128]{1,0:T(8,128)S(1)}, f32[128,128]{1,0:T(8,128)}, u32[]{:S(2)}) copy-start(f32[128,128]{1,0:T(8,128)} %stiff.7) | copy-start | bytes 196612
  15.6 5.3 %copy-start.3 = (f32[4,128,128]{2,1,0:T(8,128)S(1)}, f32[4,128,128]{2,1,0:T(8,128)}, u32[]{:S(2)}) copy-start(f32[4,128,128]{2,1,0:T(8,128)} %coupling.5) | copy-start | bytes 786436
  15.6 5.3 %copy-start.4 = (f32[32]{0:T(128)S(1)}, f32[32]{0:T(128)}, u32[]{:S(2)}) copy-start(f32[32]{0:T(128)} %reaction.7) | copy-start | bytes 388
  15.6 5.3 %copy-start.5 = (f32[32]{0:T(128)S(1)}, f32[32]{0:T(128)}, u32[]{:S(2)}) copy-start(f32[32]{0:T(128)} %axial.7) | copy-start | bytes 388
  15.6 29.7 %all-to-all-start = ((f32[8,4,128,128]{3,2,1,0:T(8,128)}), f32[8,4,128,128]{3,2,1,0:T(8,128)S(1)}, u32[]{:S(2)}, u32[]{:S(2)}) async-start(f32[8,4,128,128]{3,2,1,0:T(8,128)} %spectrum.1), calls=%async_computation | async-start | bytes 4194304 | tf_op jit(solution)/shard_map/all_to_all | solution.py:381
  21.0 1.6 %copy-start.6 = (f32[128,32,128]{2,1,0:T(8,128)S(1)}, f32[128,32,128]{2,1,0:T(8,128)}, u32[]{:S(2)}) copy-start(f32[128,32,128]{2,1,0:T(8,128)} %prev.3) | copy-start | bytes 6291460
  28.9 1.3 %copy-start = (f32[32,128,128]{2,1,0:T(8,128)}, f32[32,128,128]{2,1,0:T(8,128)S(1)}, u32[]{:S(2)}) copy-start(f32[32,128,128]{2,1,0:T(8,128)S(1)} %start.1.base) | copy-start | bytes 6291460
  45.4 1.6 %copy-start.1 = (f32[32,128,128]{2,1,0:T(8,128)S(1)}, f32[32,128,128]{2,1,0:T(8,128)}, u32[]{:S(2)}) copy-start(f32[32,128,128]{2,1,0:T(8,128)} %copy-done) | copy-start | bytes 6291460
  48.1 16.6 %collective-permute-start.2 = (f32[8,128,128]{2,1,0:T(8,128)S(1)}, f32[8,128,128]{2,1,0:T(8,128)S(1)}, u32[]{:S(2)}, u32[]{:S(2)}) collective-permute-start(f32[8,128,128]{2,1,0:T(8,128)S(1)} %get-tuple-element.16), channel_id=1, source_target_pairs={{0,8},{8,16},{16,24},{24,32},{32,40},{40,48},{48,56},{56,64},{64,7... | collective-permute-start | bytes 1572872 | tf_op jit(solution)/shard_map/ppermute | solution.py:422
  56.7 12.2 %collective-permute-start.3 = (f32[8,128,128]{2,1,0:T(8,128)S(1)}, f32[8,128,128]{2,1,0:T(8,128)S(1)}, u32[]{:S(2)}, u32[]{:S(2)}) collective-permute-start(f32[8,128,128]{2,1,0:T(8,128)S(1)} %get-tuple-element.17), channel_id=1, source_target_pairs={{8,0},{16,8},{24,16},{32,24},{40,32},{48,40},{56,48},{64,56},{72,6... | collective-permute-start | bytes 1572872 | tf_op jit(solution)/shard_map/ppermute | solution.py:423
where the time goes:
time: 72.8 us; the launch traced here: 71.7 us
  Pallas kernels  24.2 us (33%)
  starting transfers between devices  22.3 us (31%)
  waiting for transfers between devices  20.2 us (28%)
  local copies, waits for them, and re-layouts  4.61 us (6%)
    pallas_call x6, Pallas kernels, call(): pl.pallas_call(kernel, out_shape=outs, in_specs=in_specs, out_specs=out_s...  24.2 us
    all_to_all x1, waiting for transfers between devices, body(): lax.all_to_all(s, 'mode', split_axis=0, concat_axis=0, tiled=True)  15.1 us
    ppermute x1, starting transfers between devices, body(): left = lax.ppermute(tail, 'elem', to_right)  8.67 us
    ppermute x1, starting transfers between devices, body(): prev_left = lax.ppermute(tail, 'elem', to_right)  5.21 us
    unnamed x17, local copies, waits for them, and re-layouts  4.61 us
    ppermute x1, waiting for transfers between devices, body(): right = lax.ppermute(head, 'elem', to_left)  4.36 us
    all_to_all x1, starting transfers between devices, body(): lax.all_to_all(s, 'mode', split_axis=0, concat_axis=0, tiled=True)  4.36 us
    ppermute x1, starting transfers between devices, body(): right = lax.ppermute(head, 'elem', to_left)  2.1 us
  transfers between devices with their start and end apart: 5, of which 3 were waited for; matrix products, arithmetic and copies ran while one was open for 0% of the time, Pallas kernels for 26%

commit v1 on v0

v1 whole, which is shorter than its diff:
```python
import functools
import math

import jax
import jax.numpy as jnp
import numpy as np
from jax import lax
from jax.experimental import pallas as pl
from jax.experimental.pallas import tpu as pltpu
from jax.sharding import PartitionSpec as P

dt_step = 0.5
first_weight = 0.7
second_weight = 1.1

plan = (("all", 128),)


def row_starts():
    at, starts = 0, []
    for _, rows in plan:
        starts.append(at)
        at += rows
    return starts


def split(x):
    high = x.astype(jnp.bfloat16)
    low = (x - high.astype(jnp.float32)).astype(jnp.bfloat16)
    return high, low


def pair(x):
    return jnp.concatenate(split(x), axis=1)


def pair_weight(w):
    high, low = split(w)
    return jnp.concatenate(
        [jnp.concatenate([high, high], axis=1), jnp.concatenate([low, low], axis=1)], axis=0
    )


def dot_nt(x, w):
    return lax.dot_general(x, w, (((1,), (1,)), ((), ())), preferred_element_type=jnp.float32)


def times(x, w):
    y = dot_nt(x, w)
    n = y.shape[1] // 2
    return y[:, :n] + y[:, n:]


@functools.cache
def dft_tables(planes):
    half, quarter = planes // 2, planes // 4
    rows = np.arange(planes)
    waves = np.where(rows <= half, rows, rows - half)

    def table(picked, count):
        z = np.arange(count)
        phase = (waves[picked][:, None] * z[None, :]) % planes
        angle = 2.0 * np.pi / planes * phase
        t = np.where((picked <= half)[:, None], np.cos(angle), -np.sin(angle)) * planes**-0.5
        high = t.astype(np.float32).astype(jnp.bfloat16)
        low = (t - high.astype(np.float64)).astype(np.float32).astype(jnp.bfloat16)
        return np.concatenate([high, low], axis=1)

    odd = table(rows[1::2], half)
    even = np.concatenate([table(rows[2::4], quarter), table(rows[0::4], quarter)], axis=0)
    return np.concatenate([odd, even], axis=1)


def dft3(t, h, l):
    k = t.shape[1] // 2
    dot = functools.partial(jnp.dot, preferred_element_type=jnp.float32)
    return dot(t[:, :k], h) + dot(t[:, :k], l) + dot(t[:, k:], h)


def sides(meta, elems):
    rim = elems // 4
    odd = lax.rem(meta[0], 2)
    return pl.multiple_of((1 - odd) * (elems - rim), rim), pl.multiple_of(odd * (elems - rim), rim)


def by_side(meta, make):
    odd = lax.rem(meta[0], 2)

    def each(step):
        for value in range(2):

            @pl.when(odd == value)
            def _():
                for c in make(value):
                    step(c)

    return lambda: each(lambda c: c.start()), lambda: each(lambda c: c.wait())


def side_read(meta, prev, to, sems, near):
    elems = prev.shape[1]
    rows, rim, _ = to.shape
    parts = sems.shape[0]
    n = rows // parts

    def make(odd):
        at = (odd ^ near) * (elems - rim)
        return [
            pltpu.make_async_copy(
                prev.at[i * n : (i + 1) * n, at : at + rim, :], to.at[i * n : (i + 1) * n], sems.at[i]
            )
            for i in range(parts)
        ]

    return by_side(meta, make)


def pack_kernel(meta, prev, far_out, sems):
    start, wait = side_read(meta, prev, far_out, sems, 0)
    start()
    wait()


def spectrum_kernel(tile, devices, meta, far_in, prev, vel, der, table_hbm, near_out, *refs):
    outs, (table, dh, dl, eh, el, stage, sems, table_sem, near_sems) = refs[:-9], refs[-9:]
    start_near, wait_near = side_read(meta, prev, near_out, near_sems, 1)
    table_read = pltpu.make_async_copy(table_hbm, table, table_sem)
    table_read.start()
    nodes = der.shape[0]
    local = dh.shape[1] // nodes
    planes = vel.shape[0] // local
    quarter = planes // 4
    weight = pair_weight(der[...])

    for t in range(quarter // tile):
        for e in range(local):
            cols = slice(e * nodes, (e + 1) * nodes)
            v = jnp.concatenate(
                [
                    vel[pl.ds((j * quarter + t * tile) * local + e, tile, stride=local), :]
                    for j in range(4)
                ],
                axis=0,
            )
            p = v - dt_step * v * times(pair(v), weight)
            p0, p1, p2, p3 = (p[j * tile : (j + 1) * tile] for j in range(4))
            s0, s1 = p0 + p2, p1 + p3
            here, there = slice(t * tile, (t + 1) * tile), slice(quarter + t * tile, quarter + (t + 1) * tile)
            dh[here, cols], dl[here, cols] = split(p0 - p2)
            dh[there, cols], dl[there, cols] = split(p1 - p3)
            eh[here, cols], el[here, cols] = split(s0 - s1)
            eh[there, cols], el[there, cols] = split(s0 + s1)

    table_read.wait()
    start_near()
    rows = stage.shape[2]
    group, halves = 2, 2
    writes = []
    some_devices = devices // halves
    for g in range(0, local, group):
        cols = slice(g * nodes, (g + group) * nodes)
        for half in range(halves):
            m0 = half * some_devices
            for top, ph, pl_, width, offset, stride in (
                (0, dh[:, cols], dl[:, cols], slice(0, planes), 1, 2),
                (0, eh[:quarter, cols], el[:quarter, cols], slice(planes, None), 2, 4),
                (quarter, eh[quarter:, cols], el[quarter:, cols], slice(planes, None), 0, 4),
            ):
                n = rows // stride
                values = dft3(table[top + m0 * n : top + (m0 + some_devices) * n, width], ph, pl_)
                for m in range(some_devices):
                    for e in range(group):
                        stage[m0 + m, g + e, pl.ds(offset, n, stride=stride), :] = values[
                            m * n : (m + 1) * n, e * nodes : (e + 1) * nodes
                        ]
            where = (pl.ds(m0, some_devices), pl.ds(g, group))
            writes.append(
                pltpu.make_async_copy(stage.at[where], outs[0].at[where], sems.at[half, g // group])
            )
            writes[-1].start()
    wait_near()
    for c in writes:
        c.wait()


def row_shift(first_row, count, planes, lanes):
    rows = first_row + lax.broadcasted_iota(jnp.int32, (count, lanes), 0)
    half = planes // 2
    waves = jnp.where(rows <= half, rows, rows - half).astype(jnp.float32)
    return 4.0 * (waves * (1.0 / half)) ** 2


def diagonal(stiff):
    n = stiff.shape[0]
    eye = lax.broadcasted_iota(jnp.int32, (n, n), 0) == lax.broadcasted_iota(jnp.int32, (n, n), 1)
    return jnp.sum(jnp.where(eye, stiff, 0.0), axis=0, keepdims=True)


def start_kernel(planes, row_start, meta, near, reaction, axial, prev, near_in, far_in, stiff, coupling, base, far_base, out, h, y, y0, y1, sem):
    elems, rows, nodes = base.shape
    own_rows, rim, _ = near_in.shape
    group = meta[0] * elems
    prev = prev.reshape(own_rows * elems, nodes)
    near_at, far_at = sides(meta, elems)

    for side, first in ((near_in, near_at), (far_in, far_at)):
        side = side.reshape(own_rows * rim, nodes)
        place = jnp.where(first > 0, rim + elems, 0)
        for e in range(rim):
            h[place + e] = pair(side[pl.ds(row_start * rim + e, rows, stride=rim), :])
    for e in range(elems):
        v = prev[pl.ds(row_start * elems + e, rows, stride=elems), :]
        out[e] = v
        h[rim + e] = pair(v)
    step = 8

    def fill(dst, w, a, b):
        for i in range(a, b, step):
            x = h[i : i + step].reshape(step * rows, 2 * nodes)
            dst[i - a : i - a + step] = times(x, w).reshape(step, rows, nodes)

    fill(y0, pair_weight(coupling[0]), 0, rim + elems)
    fill(y1, pair_weight(coupling[1]), rim, rim + elems + rim)
    y0[rim + elems] = jnp.zeros((rows, nodes), jnp.float32)
    y1[rim + elems] = jnp.zeros((rows, nodes), jnp.float32)
    for f in (2, 3):
        fill(y.at[f - 2], pair_weight(coupling[f]), rim, rim + elems)
        y[f - 2, elems] = jnp.zeros((rows, nodes), jnp.float32)
    fill(y.at[2], pair_weight(stiff[...]), rim, rim + elems)

    shift = row_shift(meta[1] * sum(r for _, r in plan) + row_start, rows, planes, nodes)
    diag = diagonal(stiff[...])

    def place(e, f, low, high):
        n = near[e, f]
        return jnp.where(n >= 0, jnp.clip(n - group + low, 0, high - 1), high)

    def combine(e, carry):
        v = out[e]
        scaling = reaction[e] + shift * axial[e]
        total = y[2, e] + scaling * v
        total += y0[place(e, 0, rim, rim + elems)] + y1[place(e, 1, 0, rim + elems)]
        total += y[0, place(e, 2, 0, elems)] + y[1, place(e, 3, 0, elems)]
        out[e] = v - first_weight * total / (diag + scaling)
        return carry

    lax.fori_loop(0, elems, combine, 0)
    copy = pltpu.make_async_copy(out, base, sem)
    copy.start()
    for i in range(rim):
        far_base[i] = out[far_at + i]
    copy.wait()


def edge_kernel(planes, row_start, devices, meta, reaction, axial, far_base, base_hbm, rhs, stiff, near_out, far_out, near_base, sem):
    rim, rows, nodes = far_out.shape
    local = rhs.shape[1]
    elems = local * devices
    near_at, far_at = sides(meta, elems)
    read = pltpu.make_async_copy(base_hbm.at[pl.ds(near_at, rim)], near_base, sem)
    read.start()
    shift = row_shift(meta[1] * sum(r for _, r in plan) + row_start, rows, planes, nodes)
    diag = diagonal(stiff[...])
    for base, out, at in ((far_base, far_out, far_at), (near_base, near_out, near_at)):
        source = jnp.where(at > 0, (elems - rim) // local, 0)
        if base is near_base:
            read.wait()
        for i in range(rim):
            e = at + i
            inverse = 1.0 / (diag + reaction[e] + shift * axial[e])
            out[i] = base[i] + first_weight * (rhs[source + i // local, i % local] * inverse)


def second_kernel(planes, row_start, devices, meta, near, reaction, axial, base_hbm, rhs, near_in, stiff, coupling, *refs):
    out, rest, h, y, stage, sem, first, target, base, sems = refs[-10:]
    elems, rows, nodes = first.shape
    rim = rest.shape[0]
    local = elems // devices
    done = elems - rim
    group = meta[0] * elems
    near_at, far_at = sides(meta, elems)
    reads = []
    for k in range(devices):
        part = pl.ds(k * local, local)
        reads.append(pltpu.make_async_copy(base_hbm.at[part], base.at[part], sems.at[k]))
        reads[-1].start()
    shift = row_shift(meta[1] * sum(r for _, r in plan) + row_start, rows, planes, nodes)
    diag = diagonal(stiff[...])
    for e in range(rim):
        h[elems + e] = pair(near_in[e])
    for e in range(elems):
        if e % local == 0:
            reads[e // local].wait()
        r = rhs[e // local, e % local] * (1.0 / (diag + reaction[e] + shift * axial[e]))
        v = base[e] + first_weight * r
        first[e] = v
        h[e] = pair(v)
        target[e] = v + second_weight * r
    step = 8

    def fill(f, w, to=elems):
        for i in range(0, to, step):
            y[f, i : i + step] = times(h[i : i + step].reshape(step * rows, 2 * nodes), w).reshape(step, rows, nodes)

    for f in range(4):
        fill(f, pair_weight(coupling[f]), elems + rim if f < 2 else elems)
        y[f, elems + rim] = jnp.zeros((rows, nodes), jnp.float32)
    fill(4, pair_weight(stiff[...]))
    near_first = jnp.where(near_at > 0, elems, -rim)

    def place(e, f):
        n = near[e, f]
        at = n - group
        beside = at - near_first
        is_beside = (beside >= 0) & (beside < rim)
        is_own = (at >= 0) & (at < elems)
        at = jnp.where(is_own, at, jnp.where(is_beside, elems + beside, elems + rim))
        return jnp.where(n >= 0, at, elems + rim)

    def combine(e):
        v = first[e]
        scaling = reaction[e] + shift * axial[e]
        total = y[4, e] + scaling * v
        for f in range(4):
            total += y[f, place(e, f)]
        return target[e] - second_weight * total / (diag + scaling)

    lowest = pl.multiple_of(jnp.where(far_at > 0, 0, rim), rim)
    flat = stage.reshape(rows * done, nodes)
    for i in range(done):
        flat[pl.ds(i, rows, stride=done), :] = combine(lowest + i)
    start, wait = by_side(
        meta,
        lambda odd: [
            pltpu.make_async_copy(
                stage, out.at[row_start : row_start + rows, rim * (1 - odd) : rim * (1 - odd) + done, :], sem
            )
        ],
    )
    start()
    for i in range(rim):
        rest[i] = combine(far_at + i)
    wait()


def finish_kernel(planes, row_start, meta, near, reaction, axial, rest, far_in, stiff, coupling, kept, out, h, y, stage, sems):
    elems = near.shape[0]
    rim, rows, nodes = rest.shape
    group = meta[0] * elems
    _, far_at = sides(meta, elems)
    face = jnp.where(far_at > 0, 1, 0)
    far_first = group + jnp.where(far_at > 0, elems, -rim)
    parts = h.shape[0]
    n = rows // parts
    weight = pair_weight(coupling[face])
    diag = diagonal(stiff[...])
    y[rim] = jnp.zeros((n, nodes), jnp.float32)
    copies = []
    for p in range(parts):
        for e in range(rim):
            h[p, e] = pair(far_in[e, p * n : (p + 1) * n])
        y[:rim] = times(h[p].reshape(rim * n, 2 * nodes), weight).reshape(rim, n, nodes)
        first_row = row_start + p * n
        shift = row_shift(meta[1] * sum(r for _, r in plan) + first_row, n, planes, nodes)
        flat = stage.at[p].reshape(n * rim, nodes)
        for i in range(rim):
            e = far_at + i
            number = near[e, face]
            at = number - far_first
            at = jnp.where((number >= 0) & (at >= 0) & (at < rim), at, rim)
            scaling = reaction[e] + shift * axial[e]
            flat[pl.ds(i, n, stride=rim), :] = rest[i, p * n : (p + 1) * n] - second_weight * y[at] / (diag + scaling)

        def make(odd, p=p, first_row=first_row):
            at = odd * (elems - rim)
            return [pltpu.make_async_copy(stage.at[p], out.at[first_row : first_row + n, at : at + rim, :], sems.at[p])]

        copies.append(by_side(meta, make))
        copies[-1][0]()
    for _, wait in copies:
        wait()


vmem = pl.BlockSpec(memory_space=pltpu.VMEM)
smem = pl.BlockSpec(memory_space=pltpu.SMEM)
hbm = pl.BlockSpec(memory_space=pltpu.HBM)
anywhere = pl.BlockSpec(memory_space=pl.ANY)


cost = dict(edge=(4, 1), pack=(4, 1), spectrum=(24, 40), start=(24, 60), second=(28, 15), finish=(8, 2))


def call(kernel, name, outs, out_specs, in_specs, scratch, args, mib, us, aliases=None, grid=()):
    return pl.pallas_call(
        kernel,
        out_shape=outs,
        in_specs=in_specs,
        out_specs=out_specs,
        scratch_shapes=scratch,
        compiler_params=pltpu.CompilerParams(vmem_limit_bytes=mib * 2**20),
        cost_estimate=pl.CostEstimate(flops=int(us * 1e9), bytes_accessed=int(us * 3e6), transcendentals=0),
        input_output_aliases=aliases or {},
        grid=grid,
        name=name,
    )(*args)


def body(velocity, previous, derivative, stiffness, coupling, reaction, axial_weight, neighbours):
    planes, local, nodes = velocity.shape
    own_rows, elems, _ = previous.shape
    rim = elems // 4
    devices = planes // own_rows
    groups = lax.axis_size("elem")
    f32, bf16 = jnp.float32, jnp.bfloat16
    struct = jax.ShapeDtypeStruct
    vm, dma = pltpu.VMEM, pltpu.SemaphoreType.DMA
    meta = jnp.stack([lax.axis_index("elem"), lax.axis_index("mode")]).astype(jnp.int32)
    near_pairs = [(i, i ^ 1) for i in range(groups)]
    far_pairs = [p for i in range(1, groups - 1, 2) for p in ((i, i + 1), (i + 1, i))]

    def exchange(side, pairs):
        return lax.ppermute(side, "elem", pairs)

    def fixed(x, space=pltpu.VMEM):
        return pltpu.with_memory_space_constraint(x, space)

    side = (own_rows, rim, nodes)
    far_out = call(
        pack_kernel,
        "pack",
        pltpu.VMEM(side, f32),
        vmem,
        [smem, hbm],
        [dma((4,))],
        (meta, fixed(previous, pltpu.HBM)),
        *cost["pack"],
    )
    prev_far = exchange(far_out, far_pairs)

    table = dft_tables(planes)
    half, tile = planes // 2, 64
    blocks = []
    for kind, rows in plan:
        if kind == "all":
            blocks.append(pltpu.HBM((devices, local, rows, nodes), f32))
        else:
            blocks.extend([pltpu.HBM((local, rows, nodes), f32)] * devices)
    spectrum = call(
        functools.partial(spectrum_kernel, tile, devices),
        "spectrum",
        (struct(side, f32), *blocks),
        (vmem,) + (hbm,) * len(blocks),
        [smem, vmem, hbm, vmem, vmem, hbm],
        [
            vm(table.shape, bf16),
            *([vm((half, local * nodes), bf16)] * 4),
            vm((devices, local, own_rows, nodes), f32),
            dma((2, local // 2)),
            dma,
            dma((4,)),
        ],
        (
            meta, fixed(far_out), fixed(previous, pltpu.HBM),
            velocity.reshape(planes * local, nodes), derivative,
            fixed(jnp.asarray(table), pltpu.HBM),
        ),
        *cost["spectrum"],
    )
    rhs = []
    near_out, *spectrum = spectrum
    prev_near = exchange(near_out, near_pairs)
    for kind, rows in plan:
        if kind == "all":
            rhs.append([lax.all_to_all(spectrum.pop(0), "mode", split_axis=0, concat_axis=0, tiled=True)])
        else:
            rhs.append([spectrum.pop(0)])
            for k in range(1, devices):
                rhs[-1].append(lax.ppermute(spectrum.pop(0), "mode", [(m, m ^ k) for m in range(devices)]))

    scalars = (meta, neighbours, reaction, axial_weight)
    base = []
    for (_, rows), at in zip(plan, row_starts()):
        base.append(
            call(
                functools.partial(start_kernel, planes, at),
                "start",
                (pltpu.HBM((elems, rows, nodes), f32), pltpu.VMEM((rim, rows, nodes), f32)),
                (hbm, vmem),
                [smem] * 4 + [vmem] * 5,
                [
                    vm((elems, rows, nodes), f32),
                    vm((elems + 2 * rim, rows, 2 * nodes), bf16),
                    vm((3, elems + 1, rows, nodes), f32),
                    vm((elems + rim + 1, rows, nodes), f32),
                    vm((elems + rim + 1, rows, nodes), f32),
                    dma,
                ],
                (*scalars, previous, prev_near, prev_far, stiffness, coupling),
                *cost["start"],
            )
        )
    whole = struct((own_rows, elems, nodes), f32)
    out = None
    tails = []
    for c, ((_, rows), at) in enumerate(zip(plan, row_starts())):
        field = struct((elems, rows, nodes), f32)
        edge = struct((rim, rows, nodes), f32)
        base_all, base_far = base[c]
        short = (meta, reaction, axial_weight)
        near_out, far_out = call(
            functools.partial(edge_kernel, planes, at, devices),
            "edge", (edge, edge), (vmem, vmem), [smem] * 3 + [vmem, hbm, vmem, vmem], [vm((rim, rows, nodes), f32), dma],
            (*short, fixed(base_far), fixed(base_all, pltpu.HBM), *rhs[c], stiffness),
            *cost["edge"],
        )
        near_in = exchange(near_out, near_pairs)
        far_in = exchange(far_out, far_pairs)
        args = (*scalars, fixed(base_all, pltpu.HBM), *rhs[c], near_in, stiffness, coupling)
        out, rest = call(
            functools.partial(second_kernel, planes, at, devices),
            "second",
            (whole, struct((rim, rows, nodes), f32)),
            (hbm, vmem),
            [smem] * 4 + [hbm] + [vmem] * 4 + [hbm] * (out is not None),
            [
                vm((elems + rim, rows, 2 * nodes), bf16),
                vm((5, elems + rim + 1, rows, nodes), f32),
                vm((rows, elems - rim, nodes), f32),
                dma,
                *([vm((elems, rows, nodes), f32)] * 3),
                dma((devices,)),
            ],
            args if out is None else (*args, out),
            *cost["second"],
            aliases=None if out is None else {len(args): 0},
        )
        tails.append((rows, at, rest, far_in))
    for rows, at, rest, far_in in tails:
        args = (*scalars, rest, far_in, stiffness, coupling, out)
        out = call(
            functools.partial(finish_kernel, planes, at),
            "finish",
            whole,
            hbm,
            [smem] * 4 + [vmem] * 4 + [hbm],
            [
                vm((4, rim, rows // 4, 2 * nodes), bf16),
                vm((rim + 1, rows // 4, nodes), f32),
                vm((4, rows // 4, rim, nodes), f32),
                dma((4,)),
            ],
            args,
            *cost["finish"],
            aliases={len(args) - 1: 0},
        )
    return out


def solution(mesh):
    return jax.shard_map(
        body,
        mesh=mesh,
        in_specs=(
            P(None, ("elem", "mode"), None),
            P("mode", "elem", None),
            P(),
            P(),
            P(),
            P("elem"),
            P("elem"),
            P("elem", None),
        ),
        out_specs=P("mode", "elem", None),
        check_vma=False,
    )
```

time: 72.8 us -> 68 us (0.934)
  starting transfers between devices: 22.3 us -> 17.4 us
  Pallas kernels: 24.2 us -> 27.2 us
  local copies, waits for them, and re-layouts: 4.61 us -> 1.71 us
    ppermute x4, starting transfers between devices: 17.9 us -> 13.1 us  [exchange(): return lax.ppermute(side, 'elem', pairs)]
    pallas_call x6, Pallas kernels: 24.2 us -> 27.2 us  [call(): pl.pallas_call(kernel, out_shape=outs, in_specs=in_specs, out_specs=out_s...]
    unnamed x17, local copies, waits for them, and re-layouts: 4.61 us -> 1.71 us
    ppermute x4, waiting for transfers between devices: 5.12 us -> 5.86 us  [exchange(): return lax.ppermute(side, 'elem', pairs)]
  transfers between devices with their start and end apart: 5 -> 5, of which waited for: 3 -> 3; matrix products, arithmetic and copies ran while one was open for 0% -> 0% of each run, Pallas kernels for 26% -> 32%
where the time goes in v1:
time: 68 us; the launch traced here: 67 us
  Pallas kernels  27.2 us (40%)
  waiting for transfers between devices  20.3 us (30%)
  starting transfers between devices  17.4 us (26%)
  local copies, waits for them, and re-layouts  1.71 us (3%)
    pallas_call x6, Pallas kernels, call(): pl.pallas_call(kernel, out_shape=outs, in_specs=in_specs, out_specs=out_s...  27.2 us
    all_to_all x1, waiting for transfers between devices, body(): lax.all_to_all(spectrum.pop(0), 'mode', split_axis=0, concat_axis=0, tile...  14.5 us
    ppermute x4, starting transfers between devices, exchange(): return lax.ppermute(side, 'elem', pairs)  13.1 us
    ppermute x4, waiting for transfers between devices, exchange(): return lax.ppermute(side, 'elem', pairs)  5.86 us
    all_to_all x1, starting transfers between devices, body(): lax.all_to_all(spectrum.pop(0), 'mode', split_axis=0, concat_axis=0, tile...  4.36 us
    unnamed x17, local copies, waits for them, and re-layouts  1.71 us
  transfers between devices with their start and end apart: 5, of which 3 were waited for; matrix products, arithmetic and copies ran while one was open for 0% of the time, Pallas kernels for 32%

profile of v1, /device:TPU:97, one launch (start us, length us, event | category | flops | bytes accessed | tf_op | source)
XLA Modules:
  0.0 67.0 jit_solution(10300033033119197806)
XLA Ops:
  0.0 0.1 pad_add_fusion.meta
  0.1 1.7 %pack.1.far_in = f32[128,8,128]{2,1,0:T(8,128)S(1)} custom-call(s32[2]{0:T(128)S(1)} %pad_add_fusion.meta, f32[128,32,128]{2,1,0:T(8,128)} %prev.5), custom_call_target="tpu_custom_call" | custom-call | flops 1000000000 | bytes 3000000 | tf_op jit(solution)/shard_map/pack/pallas_call | solution.py:394
  1.8 5.2 %collective-permute-start.1 = (f32[128,8,128]{2,1,0:T(8,128)S(1)}, f32[128,8,128]{2,1,0:T(8,128)S(1)}, u32[]{:S(2)}, u32[]{:S(2)}) collective-permute-start(f32[128,8,128]{2,1,0:T(8,128)S(1)} %pack.1.far_in), channel_id=1, source_target_pairs={{8,16},{16,8},{24,32},{32,24},{40,48},{48,40},{56,64},{64,56},{72,... | collective-permute-start | bytes 1572872 | tf_op jit(solution)/shard_map/ppermute | solution.py:422
  7.0 5.5 %spectrum.1 = (f32[128,8,128]{2,1,0:T(8,128)}, f32[8,4,128,128]{3,2,1,0:T(8,128)}) custom-call(s32[2]{0:T(128)S(1)} %pad_add_fusion.meta, f32[128,8,128]{2,1,0:T(8,128)S(1)} %pack.1.far_in, f32[128,32,128]{2,1,0:T(8,128)} %prev.5, f32[4096,128]{1,0:T(8,128)S(1)} %bitcast.3, f32[128,128]{1,0:T(8,128)S(1)} %copy-done.6, bf16[512,1536]{1,0:T(8,128)(2,1)} %constant.11.clone.table_hbm), custom_call_target="tpu_custom_call" | custom-call | flops 40000000000 | bytes 120000000 | tf_op jit(solution)/shard_map/spectrum/pallas_call | solution.py:394
  12.6 0.1 collective-permute-start
  12.7 0.0 copy-start.7
  12.7 0.0 copy-start
  12.7 0.0 copy-start.1
  12.7 0.0 copy-start.2
  12.7 0.0 copy-start.5
  12.7 4.4 %all-to-all-start = ((f32[8,4,128,128]{3,2,1,0:T(8,128)}), f32[8,4,128,128]{3,2,1,0:T(8,128)S(1)}, u32[]{:S(2)}, u32[]{:S(2)}) async-start(f32[8,4,128,128]{3,2,1,0:T(8,128)} %get-tuple-element.15), calls=%async_computation | async-start | bytes 4194304 | tf_op jit(solution)/shard_map/all_to_all | solution.py:474
  17.1 0.1 copy.13.near
  17.2 2.3 %collective-permute-done.1.far_in = f32[128,8,128]{2,1,0:T(8,128)S(1)} collective-permute-done((f32[128,8,128]{2,1,0:T(8,128)S(1)}, f32[128,8,128]{2,1,0:T(8,128)S(1)}, u32[]{:S(2)}, u32[]{:S(2)}) %collective-permute-start.1) | collective-permute-done | bytes 524320 | tf_op jit(solution)/shard_map/ppermute | solution.py:422
  19.5 0.0 collective-permute-done.near_in
  19.5 0.0 copy-start.4
  19.5 1.6 %copy-done.4 = f32[128,32,128]{2,1,0:T(8,128)S(1)} copy-done((f32[128,32,128]{2,1,0:T(8,128)S(1)}, f32[128,32,128]{2,1,0:T(8,128)}, u32[]{:S(2)}) %copy-start.4) | copy-done | bytes 2097176
  21.1 8.0 %start.1 = (f32[32,128,128]{2,1,0:T(8,128)}, f32[8,128,128]{2,1,0:T(8,128)S(1)}) custom-call(s32[2]{0:T(128)S(1)} %pad_add_fusion.meta, s32[32,4]{1,0:T(8,128)S(1)} %copy.13.near, f32[32]{0:T(128)S(1)} %copy-done.1, f32[32]{0:T(128)S(1)} %copy-done.2, f32[128,32,128]{2,1,0:T(8,128)S(1)} %copy-done.4, f32[128,8,128]{2,1,0:T(8,128)} %collective-permute-done.near_in, ...), custom_call_target="tpu_custom_call" | custom-call | flops 60000002048 | bytes 180000000 | tf_op jit(solution)/shard_map/start/pallas_call | solution.py:394
  29.2 14.5 %all-to-all-done.rhs = f32[8,4,128,128]{3,2,1,0:T(8,128)S(1)} async-done(((f32[8,4,128,128]{3,2,1,0:T(8,128)}), f32[8,4,128,128]{3,2,1,0:T(8,128)S(1)}, u32[]{:S(2)}, u32[]{:S(2)}) %all-to-all-start) | async-done | bytes 2097184 | tf_op jit(solution)/shard_map/all_to_all | solution.py:474
  43.6 1.7 %edge.1 = (f32[8,128,128]{2,1,0:T(8,128)S(1)}, f32[8,128,128]{2,1,0:T(8,128)S(1)}) custom-call(s32[2]{0:T(128)S(1)} %pad_add_fusion.meta, f32[32]{0:T(128)S(1)} %copy-done.1, f32[32]{0:T(128)S(1)} %copy-done.2, f32[8,128,128]{2,1,0:T(8,128)S(1)} %get-tuple-element.16.far_base, f32[32,128,128]{2,1,0:T(8,128)} %get-tuple-element.14.base_hbm, ...), custom_call_target="tpu_custom_call" | custom-call | flops 1000000000 | bytes 3000000 | tf_op jit(solution)/shard_map/edge/pallas_call | solution.py:394
  45.4 1.6 %collective-permute-start.2 = (f32[8,128,128]{2,1,0:T(8,128)S(1)}, f32[8,128,128]{2,1,0:T(8,128)S(1)}, u32[]{:S(2)}, u32[]{:S(2)}) collective-permute-start(f32[8,128,128]{2,1,0:T(8,128)S(1)} %get-tuple-element.17), channel_id=1, source_target_pairs={{0,8},{8,0},{16,24},{24,16},{32,40},{40,32},{48,56},{56,48},{64,72... | collective-permute-start | bytes 1572872 | tf_op jit(solution)/shard_map/ppermute | solution.py:422
  47.0 6.1 %collective-permute-start.3 = (f32[8,128,128]{2,1,0:T(8,128)S(1)}, f32[8,128,128]{2,1,0:T(8,128)S(1)}, u32[]{:S(2)}, u32[]{:S(2)}) collective-permute-start(f32[8,128,128]{2,1,0:T(8,128)S(1)} %get-tuple-element.19), channel_id=1, source_target_pairs={{8,16},{16,8},{24,32},{32,24},{40,48},{48,40},{56,64},{64,56},{72,... | collective-permute-start | bytes 1572872 | tf_op jit(solution)/shard_map/ppermute | solution.py:422
  53.2 8.1 %second.1 = (f32[128,32,128]{2,1,0:T(8,128)}, f32[8,128,128]{2,1,0:T(8,128)S(1)}) custom-call(s32[2]{0:T(128)S(1)} %pad_add_fusion.meta, s32[32,4]{1,0:T(8,128)S(1)} %copy.13.near, f32[32]{0:T(128)S(1)} %copy-done.1, f32[32]{0:T(128)S(1)} %copy-done.2, f32[32,128,128]{2,1,0:T(8,128)} %get-tuple-element.14.base_hbm, f32[8,4,128,128]{3,2,1,0:T(8,128)S(1)} %all-to-all-done.rhs, ...), custom_call_target="tpu_custom_call" | custom-call | flops 15000000512 | bytes 45000000 | tf_op jit(solution)/shard_map/second/pallas_call | solution.py:394
  61.3 3.5 %collective-permute-done.3.far_in = f32[8,128,128]{2,1,0:T(8,128)S(1)} collective-permute-done((f32[8,128,128]{2,1,0:T(8,128)S(1)}, f32[8,128,128]{2,1,0:T(8,128)S(1)}, u32[]{:S(2)}, u32[]{:S(2)}) %collective-permute-start.3) | collective-permute-done | bytes 524320 | tf_op jit(solution)/shard_map/ppermute | solution.py:422
  64.8 2.0 %finish.1 = f32[128,32,128]{2,1,0:T(8,128)} custom-call(s32[2]{0:T(128)S(1)} %pad_add_fusion.meta, s32[32,4]{1,0:T(8,128)S(1)} %copy.13.near, f32[32]{0:T(128)S(1)} %copy-done.1, f32[32]{0:T(128)S(1)} %copy-done.2, f32[8,128,128]{2,1,0:T(8,128)S(1)} %get-tuple-element.18.rest, ...), custom_call_target="tpu_custom_call", output_to_operand_aliasing={{}: (8, {})} | custom-call | flops 2000000000 | bytes 6000000 | tf_op jit(solution)/shard_map/finish/pallas_call | solution.py:394
  (10 shorter events, 0.0 us)
Async XLA Ops:
  0.0 7.0 %copy-start.6 = (f32[128,128]{1,0:T(8,128)S(1)}, f32[128,128]{1,0:T(8,128)}, u32[]{:S(2)}) copy-start(f32[128,128]{1,0:T(8,128)} %der.1) | copy-start | bytes 196612
  0.0 7.0 %copy-start.3 = (f32[1024,4,128]{2,1,0:T(4,128)S(1)}, f32[1024,4,128]{2,1,0:T(4,128)}, u32[]{:S(2)}) copy-start(f32[1024,4,128]{2,1,0:T(4,128)} %param.9) | copy-start | bytes 6291460
  1.8 17.7 %collective-permute-start.1 = (f32[128,8,128]{2,1,0:T(8,128)S(1)}, f32[128,8,128]{2,1,0:T(8,128)S(1)}, u32[]{:S(2)}, u32[]{:S(2)}) collective-permute-start(f32[128,8,128]{2,1,0:T(8,128)S(1)} %pack.1.far_in), channel_id=1, source_target_pairs={{8,16},{16,8},{24,32},{32,24},{40,48},{48,40},{56,64},{64,56},{72,... | collective-permute-start | bytes 1572872 | tf_op jit(solution)/shard_map/ppermute | solution.py:422
  12.6 6.9 %collective-permute-start = (f32[128,8,128]{2,1,0:T(8,128)}, f32[128,8,128]{2,1,0:T(8,128)}, u32[]{:S(2)}, u32[]{:S(2)}) collective-permute-start(f32[128,8,128]{2,1,0:T(8,128)} %get-tuple-element.13), channel_id=1, source_target_pairs={{0,8},{8,0},{16,24},{24,16},{32,40},{40,32},{48,56},{56,48},{64,72... | collective-permute-start | bytes 1572872 | tf_op jit(solution)/shard_map/ppermute | solution.py:422
  12.7 4.4 %copy-start.7 = (s32[32,4]{0,1:T(4,128)S(1)}, s32[32,4]{0,1:T(4,128)}, u32[]{:S(2)}) copy-start(s32[32,4]{0,1:T(4,128)} %param.16) | copy-start | bytes 1540
  12.7 6.8 %copy-start = (f32[128,128]{1,0:T(8,128)S(1)}, f32[128,128]{1,0:T(8,128)}, u32[]{:S(2)}) copy-start(f32[128,128]{1,0:T(8,128)} %stiff.7) | copy-start | bytes 196612
  12.7 6.8 %copy-start.1 = (f32[32]{0:T(128)S(1)}, f32[32]{0:T(128)}, u32[]{:S(2)}) copy-start(f32[32]{0:T(128)} %reaction.7) | copy-start | bytes 388
  12.7 6.8 %copy-start.2 = (f32[32]{0:T(128)S(1)}, f32[32]{0:T(128)}, u32[]{:S(2)}) copy-start(f32[32]{0:T(128)} %axial.7) | copy-start | bytes 388
  12.7 6.8 %copy-start.5 = (f32[4,128,128]{2,1,0:T(8,128)S(1)}, f32[4,128,128]{2,1,0:T(8,128)}, u32[]{:S(2)}) copy-start(f32[4,128,128]{2,1,0:T(8,128)} %coupling.5) | copy-start | bytes 786436
  12.7 30.9 %all-to-all-start = ((f32[8,4,128,128]{3,2,1,0:T(8,128)}), f32[8,4,128,128]{3,2,1,0:T(8,128)S(1)}, u32[]{:S(2)}, u32[]{:S(2)}) async-start(f32[8,4,128,128]{3,2,1,0:T(8,128)} %get-tuple-element.15), calls=%async_computation | async-start | bytes 4194304 | tf_op jit(solution)/shard_map/all_to_all | solution.py:474
  19.5 1.6 %copy-start.4 = (f32[128,32,128]{2,1,0:T(8,128)S(1)}, f32[128,32,128]{2,1,0:T(8,128)}, u32[]{:S(2)}) copy-start(f32[128,32,128]{2,1,0:T(8,128)} %prev.5) | copy-start | bytes 6291460
  45.4 7.8 %collective-permute-start.2 = (f32[8,128,128]{2,1,0:T(8,128)S(1)}, f32[8,128,128]{2,1,0:T(8,128)S(1)}, u32[]{:S(2)}, u32[]{:S(2)}) collective-permute-start(f32[8,128,128]{2,1,0:T(8,128)S(1)} %get-tuple-element.17), channel_id=1, source_target_pairs={{0,8},{8,0},{16,24},{24,16},{32,40},{40,32},{48,56},{56,48},{64,72... | collective-permute-start | bytes 1572872 | tf_op jit(solution)/shard_map/ppermute | solution.py:422
  47.0 17.8 %collective-permute-start.3 = (f32[8,128,128]{2,1,0:T(8,128)S(1)}, f32[8,128,128]{2,1,0:T(8,128)S(1)}, u32[]{:S(2)}, u32[]{:S(2)}) collective-permute-start(f32[8,128,128]{2,1,0:T(8,128)S(1)} %get-tuple-element.19), channel_id=1, source_target_pairs={{8,16},{16,8},{24,32},{32,24},{40,48},{48,40},{56,64},{64,56},{72,... | collective-permute-start | bytes 1572872 | tf_op jit(solution)/shard_map/ppermute | solution.py:422

commit v2 on v1

--- a/solution.py
+++ b/solution.py
@@ -68,7 +68,7 @@
 
     odd = table(rows[1::2], half)
     even = np.concatenate([table(rows[2::4], quarter), table(rows[0::4], quarter)], axis=0)
-    return np.concatenate([odd, even], axis=1)
+    return odd, even
 
 
 def dft3(t, h, l):
@@ -121,11 +121,12 @@
     wait()
 
 
-def spectrum_kernel(tile, devices, meta, far_in, prev, vel, der, table_hbm, near_out, *refs):
-    outs, (table, dh, dl, eh, el, stage, sems, table_sem, near_sems) = refs[:-9], refs[-9:]
+def spectrum_kernel(tile, devices, meta, far_in, prev, vel, der, odd_table, even_hbm, near_out, *refs):
+    outs, (even_table, dh, dl, eh, el, stage, sems, table_sem, near_sems) = refs[:-9], refs[-9:]
     start_near, wait_near = side_read(meta, prev, near_out, near_sems, 1)
-    table_read = pltpu.make_async_copy(table_hbm, table, table_sem)
+    table_read = pltpu.make_async_copy(even_hbm, even_table, table_sem)
     table_read.start()
+    start_near()
     nodes = der.shape[0]
     local = dh.shape[1] // nodes
     planes = vel.shape[0] // local
@@ -152,7 +153,6 @@
             eh[there, cols], el[there, cols] = split(s0 + s1)
 
     table_read.wait()
-    start_near()
     rows = stage.shape[2]
     group, halves = 2, 2
     writes = []
@@ -161,13 +161,13 @@
         cols = slice(g * nodes, (g + group) * nodes)
         for half in range(halves):
             m0 = half * some_devices
-            for top, ph, pl_, width, offset, stride in (
-                (0, dh[:, cols], dl[:, cols], slice(0, planes), 1, 2),
-                (0, eh[:quarter, cols], el[:quarter, cols], slice(planes, None), 2, 4),
-                (quarter, eh[quarter:, cols], el[quarter:, cols], slice(planes, None), 0, 4),
+            for table, top, high, low, offset, stride in (
+                (odd_table, 0, dh[:, cols], dl[:, cols], 1, 2),
+                (even_table, 0, eh[:quarter, cols], el[:quarter, cols], 2, 4),
+                (even_table, quarter, eh[quarter:, cols], el[quarter:, cols], 0, 4),
             ):
                 n = rows // stride
-                values = dft3(table[top + m0 * n : top + (m0 + some_devices) * n, width], ph, pl_)
+                values = dft3(table[top + m0 * n : top + (m0 + some_devices) * n], high, low)
                 for m in range(some_devices):
                     for e in range(group):
                         stage[m0 + m, g + e, pl.ds(offset, n, stride=stride), :] = values[
@@ -252,31 +252,39 @@
     copy.wait()
 
 
-def edge_kernel(planes, row_start, devices, meta, reaction, axial, far_base, base_hbm, rhs, stiff, near_out, far_out, near_base, sem):
-    rim, rows, nodes = far_out.shape
+def edge_kernel(planes, row_start, devices, near, meta, reaction, axial, base_in, rhs, stiff, *refs):
+    out, *refs = refs[1:] if near else refs
+    rim, rows, nodes = out.shape
     local = rhs.shape[1]
     elems = local * devices
-    near_at, far_at = sides(meta, elems)
-    read = pltpu.make_async_copy(base_hbm.at[pl.ds(near_at, rim)], near_base, sem)
-    read.start()
+    at = sides(meta, elems)[0 if near else 1]
+    base, reads = base_in, []
+    if near:
+        base, sems = refs
+        parts = sems.shape[0]
+        n = rim // parts
+        for p in range(parts):
+            reads.append(
+                pltpu.make_async_copy(base_in.at[pl.ds(at + p * n, n)], base.at[pl.ds(p * n, n)], sems.at[p])
+            )
+            reads[-1].start()
     shift = row_shift(meta[1] * sum(r for _, r in plan) + row_start, rows, planes, nodes)
     diag = diagonal(stiff[...])
-    for base, out, at in ((far_base, far_out, far_at), (near_base, near_out, near_at)):
-        source = jnp.where(at > 0, (elems - rim) // local, 0)
-        if base is near_base:
-            read.wait()
-        for i in range(rim):
-            e = at + i
-            inverse = 1.0 / (diag + reaction[e] + shift * axial[e])
-            out[i] = base[i] + first_weight * (rhs[source + i // local, i % local] * inverse)
-
-
-def second_kernel(planes, row_start, devices, meta, near, reaction, axial, base_hbm, rhs, near_in, stiff, coupling, *refs):
-    out, rest, h, y, stage, sem, first, target, base, sems = refs[-10:]
+    source = jnp.where(at > 0, (elems - rim) // local, 0)
+    for i in range(rim):
+        if near and i % n == 0:
+            reads[i // n].wait()
+        e = at + i
+        inverse = 1.0 / (diag + reaction[e] + shift * axial[e])
+        out[i] = base[i] + first_weight * (rhs[source + i // local, i % local] * inverse)
+
+
+def second_kernel(planes, row_start, devices, meta, near, reaction, axial, base_hbm, rhs, stiff, coupling, *refs):
+    out, near_rest, far_rest, h, y, stage, sem, first, target, base, sems = refs[-11:]
     elems, rows, nodes = first.shape
-    rim = rest.shape[0]
+    rim = far_rest.shape[0]
     local = elems // devices
-    done = elems - rim
+    done = elems - 2 * rim
     group = meta[0] * elems
     near_at, far_at = sides(meta, elems)
     reads = []
@@ -286,8 +294,6 @@
         reads[-1].start()
     shift = row_shift(meta[1] * sum(r for _, r in plan) + row_start, rows, planes, nodes)
     diag = diagonal(stiff[...])
-    for e in range(rim):
-        h[elems + e] = pair(near_in[e])
     for e in range(elems):
         if e % local == 0:
             reads[e // local].wait()
@@ -298,24 +304,18 @@
         target[e] = v + second_weight * r
     step = 8
 
-    def fill(f, w, to=elems):
-        for i in range(0, to, step):
+    def fill(f, w):
+        for i in range(0, elems, step):
             y[f, i : i + step] = times(h[i : i + step].reshape(step * rows, 2 * nodes), w).reshape(step, rows, nodes)
 
     for f in range(4):
-        fill(f, pair_weight(coupling[f]), elems + rim if f < 2 else elems)
-        y[f, elems + rim] = jnp.zeros((rows, nodes), jnp.float32)
+        fill(f, pair_weight(coupling[f]))
+        y[f, elems] = jnp.zeros((rows, nodes), jnp.float32)
     fill(4, pair_weight(stiff[...]))
-    near_first = jnp.where(near_at > 0, elems, -rim)
 
     def place(e, f):
-        n = near[e, f]
-        at = n - group
-        beside = at - near_first
-        is_beside = (beside >= 0) & (beside < rim)
-        is_own = (at >= 0) & (at < elems)
-        at = jnp.where(is_own, at, jnp.where(is_beside, elems + beside, elems + rim))
-        return jnp.where(n >= 0, at, elems + rim)
+        at = near[e, f] - group
+        return jnp.where((at >= 0) & (at < elems), at, elems)
 
     def combine(e):
         v = first[e]
@@ -325,31 +325,24 @@
             total += y[f, place(e, f)]
         return target[e] - second_weight * total / (diag + scaling)
 
-    lowest = pl.multiple_of(jnp.where(far_at > 0, 0, rim), rim)
     flat = stage.reshape(rows * done, nodes)
     for i in range(done):
-        flat[pl.ds(i, rows, stride=done), :] = combine(lowest + i)
-    start, wait = by_side(
-        meta,
-        lambda odd: [
-            pltpu.make_async_copy(
-                stage, out.at[row_start : row_start + rows, rim * (1 - odd) : rim * (1 - odd) + done, :], sem
-            )
-        ],
-    )
-    start()
+        flat[pl.ds(i, rows, stride=done), :] = combine(rim + i)
+    copy = pltpu.make_async_copy(stage, out.at[row_start : row_start + rows, rim : rim + done, :], sem)
+    copy.start()
     for i in range(rim):
-        rest[i] = combine(far_at + i)
-    wait()
-
-
-def finish_kernel(planes, row_start, meta, near, reaction, axial, rest, far_in, stiff, coupling, kept, out, h, y, stage, sems):
+        near_rest[i] = combine(near_at + i)
+        far_rest[i] = combine(far_at + i)
+    copy.wait()
+
+
+def finish_kernel(planes, row_start, side, meta, near, reaction, axial, rest, beside, stiff, coupling, kept, out, h, y, stage, sems):
     elems = near.shape[0]
-    rim, rows, nodes = rest.shape
+    rim, rows, nodes = beside.shape
     group = meta[0] * elems
-    _, far_at = sides(meta, elems)
-    face = jnp.where(far_at > 0, 1, 0)
-    far_first = group + jnp.where(far_at > 0, elems, -rim)
+    column = sides(meta, elems)[side]
+    face = jnp.where(column > 0, 1, 0)
+    beside_first = group + jnp.where(column > 0, elems, -rim)
     parts = h.shape[0]
     n = rows // parts
     weight = pair_weight(coupling[face])
@@ -358,21 +351,21 @@
     copies = []
     for p in range(parts):
         for e in range(rim):
-            h[p, e] = pair(far_in[e, p * n : (p + 1) * n])
+            h[p, e] = pair(beside[e, p * n : (p + 1) * n])
         y[:rim] = times(h[p].reshape(rim * n, 2 * nodes), weight).reshape(rim, n, nodes)
         first_row = row_start + p * n
         shift = row_shift(meta[1] * sum(r for _, r in plan) + first_row, n, planes, nodes)
         flat = stage.at[p].reshape(n * rim, nodes)
         for i in range(rim):
-            e = far_at + i
+            e = column + i
             number = near[e, face]
-            at = number - far_first
+            at = number - beside_first
             at = jnp.where((number >= 0) & (at >= 0) & (at < rim), at, rim)
             scaling = reaction[e] + shift * axial[e]
             flat[pl.ds(i, n, stride=rim), :] = rest[i, p * n : (p + 1) * n] - second_weight * y[at] / (diag + scaling)
 
         def make(odd, p=p, first_row=first_row):
-            at = odd * (elems - rim)
+            at = (odd ^ (1 - side)) * (elems - rim)
             return [pltpu.make_async_copy(stage.at[p], out.at[first_row : first_row + n, at : at + rim, :], sems.at[p])]
 
         copies.append(by_side(meta, make))
@@ -387,7 +380,7 @@
 anywhere = pl.BlockSpec(memory_space=pl.ANY)
 
 
-cost = dict(edge=(4, 1), pack=(4, 1), spectrum=(24, 40), start=(24, 60), second=(28, 15), finish=(8, 2))
+cost = dict(far_edge=(4, 1), near_edge=(4, 1), pack=(4, 1), spectrum=(24, 40), start=(24, 60), second=(28, 15), finish=(8, 2))
 
 
 def call(kernel, name, outs, out_specs, in_specs, scratch, args, mib, us, aliases=None, grid=()):
@@ -437,7 +430,7 @@
     )
     prev_far = exchange(far_out, far_pairs)
 
-    table = dft_tables(planes)
+    odd_table, even_table = dft_tables(planes)
     half, tile = planes // 2, 64
     blocks = []
     for kind, rows in plan:
@@ -450,9 +443,9 @@
         "spectrum",
         (struct(side, f32), *blocks),
         (vmem,) + (hbm,) * len(blocks),
-        [smem, vmem, hbm, vmem, vmem, hbm],
+        [smem, vmem, hbm, vmem, vmem, vmem, hbm],
         [
-            vm(table.shape, bf16),
+            vm(even_table.shape, bf16),
             *([vm((half, local * nodes), bf16)] * 4),
             vm((devices, local, own_rows, nodes), f32),
             dma((2, local // 2)),
@@ -462,7 +455,7 @@
         (
             meta, fixed(far_out), fixed(previous, pltpu.HBM),
             velocity.reshape(planes * local, nodes), derivative,
-            fixed(jnp.asarray(table), pltpu.HBM),
+            jnp.asarray(odd_table), fixed(jnp.asarray(even_table), pltpu.HBM),
         ),
         *cost["spectrum"],
     )
@@ -500,59 +493,61 @@
             )
         )
     whole = struct((own_rows, elems, nodes), f32)
-    out = None
-    tails = []
     for c, ((_, rows), at) in enumerate(zip(plan, row_starts())):
         field = struct((elems, rows, nodes), f32)
         edge = struct((rim, rows, nodes), f32)
         base_all, base_far = base[c]
+        base_all = fixed(base_all, pltpu.HBM)
         short = (meta, reaction, axial_weight)
-        near_out, far_out = call(
-            functools.partial(edge_kernel, planes, at, devices),
-            "edge", (edge, edge), (vmem, vmem), [smem] * 3 + [vmem, hbm, vmem, vmem], [vm((rim, rows, nodes), f32), dma],
-            (*short, fixed(base_far), fixed(base_all, pltpu.HBM), *rhs[c], stiffness),
-            *cost["edge"],
+        far_out = call(
+            functools.partial(edge_kernel, planes, at, devices, False),
+            "far_edge", edge, vmem, [smem] * 3 + [vmem] * 3, [], (*short, fixed(base_far), *rhs[c], stiffness),
+            *cost["far_edge"],
+        )
+        far_in = exchange(far_out, far_pairs)
+        near_out = call(
+            functools.partial(edge_kernel, planes, at, devices, True),
+            "near_edge", edge, vmem, [smem] * 3 + [hbm] + [vmem] * 3, [vm((rim, rows, nodes), f32), dma((4,))],
+            (*short, base_all, *rhs[c], stiffness, far_out),
+            *cost["near_edge"],
         )
         near_in = exchange(near_out, near_pairs)
-        far_in = exchange(far_out, far_pairs)
-        args = (*scalars, fixed(base_all, pltpu.HBM), *rhs[c], near_in, stiffness, coupling)
-        out, rest = call(
+        out, near_rest, far_rest = call(
             functools.partial(second_kernel, planes, at, devices),
             "second",
-            (whole, struct((rim, rows, nodes), f32)),
-            (hbm, vmem),
-            [smem] * 4 + [hbm] + [vmem] * 4 + [hbm] * (out is not None),
+            (whole, edge, edge),
+            (hbm, vmem, vmem),
+            [smem] * 4 + [hbm] + [vmem] * 3,
             [
-                vm((elems + rim, rows, 2 * nodes), bf16),
-                vm((5, elems + rim + 1, rows, nodes), f32),
-                vm((rows, elems - rim, nodes), f32),
+                vm((elems, rows, 2 * nodes), bf16),
+                vm((5, elems + 1, rows, nodes), f32),
+                vm((rows, elems - 2 * rim, nodes), f32),
                 dma,
                 *([vm((elems, rows, nodes), f32)] * 3),
                 dma((devices,)),
             ],
-            args if out is None else (*args, out),
+            (*scalars, base_all, *rhs[c], stiffness, coupling),
             *cost["second"],
-            aliases=None if out is None else {len(args): 0},
         )
-        tails.append((rows, at, rest, far_in))
-    for rows, at, rest, far_in in tails:
-        args = (*scalars, rest, far_in, stiffness, coupling, out)
-        out = call(
-            functools.partial(finish_kernel, planes, at),
-            "finish",
-            whole,
-            hbm,
-            [smem] * 4 + [vmem] * 4 + [hbm],
-            [
-                vm((4, rim, rows // 4, 2 * nodes), bf16),
-                vm((rim + 1, rows // 4, nodes), f32),
-                vm((4, rows // 4, rim, nodes), f32),
-                dma((4,)),
-            ],
-            args,
-            *cost["finish"],
-            aliases={len(args) - 1: 0},
-        )
+        for side, (rest, beside) in enumerate(((near_rest, near_in), (far_rest, far_in))):
+            args = (*scalars, rest, beside, stiffness, coupling, out)
+            parts = 4
+            out = call(
+                functools.partial(finish_kernel, planes, at, side),
+                "near_finish" if side == 0 else "far_finish",
+                whole,
+                hbm,
+                [smem] * 4 + [vmem] * 4 + [hbm],
+                [
+                    vm((parts, rim, rows // parts, 2 * nodes), bf16),
+                    vm((rim + 1, rows // parts, nodes), f32),
+                    vm((parts, rows // parts, rim, nodes), f32),
+                    dma((parts,)),
+                ],
+                args,
+                *cost["finish"],
+                aliases={len(args) - 1: 0},
+            )
     return out
 
 

time: 68 us -> 66.5 us (0.978)
  Pallas kernels: 27.2 us -> 29.3 us
  waiting for transfers between devices: 20.3 us -> 18.5 us
  starting transfers between devices: 17.4 us -> 16.3 us
    ppermute x4, waiting for transfers between devices: 5.86 us -> 3.46 us  [exchange(): return lax.ppermute(side, 'elem', pairs)]
    pallas_call x6 -> x8, Pallas kernels: 27.2 us -> 29.3 us  [call(): pl.pallas_call(kernel, out_shape=outs, in_specs=in_specs, out_specs=out_s...]
    ppermute x4, starting transfers between devices: 13.1 us -> 11.9 us  [exchange(): return lax.ppermute(side, 'elem', pairs)]
    unnamed x17 -> x19, local copies, waits for them, and re-layouts: 1.71 us -> 1.72 us
  transfers between devices with their start and end apart: 5 -> 5, of which waited for: 3 -> 3; matrix products, arithmetic and copies ran while one was open for 0% -> 0% of each run, Pallas kernels for 32% -> 37%
where the time goes in v2:
time: 66.5 us; the launch traced here: 66.2 us
  Pallas kernels  29.3 us (44%)
  waiting for transfers between devices  18.5 us (28%)
  starting transfers between devices  16.3 us (25%)
  local copies, waits for them, and re-layouts  1.72 us (3%)
    pallas_call x8, Pallas kernels, call(): pl.pallas_call(kernel, out_shape=outs, in_specs=in_specs, out_specs=out_s...  29.3 us
    all_to_all x1, waiting for transfers between devices, body(): lax.all_to_all(spectrum.pop(0), 'mode', split_axis=0, concat_axis=0, tile...  15 us
    ppermute x4, starting transfers between devices, exchange(): return lax.ppermute(side, 'elem', pairs)  11.9 us
    all_to_all x1, starting transfers between devices, body(): lax.all_to_all(spectrum.pop(0), 'mode', split_axis=0, concat_axis=0, tile...  4.36 us
    ppermute x4, waiting for transfers between devices, exchange(): return lax.ppermute(side, 'elem', pairs)  3.46 us
    unnamed x19, local copies, waits for them, and re-layouts  1.72 us
  transfers between devices with their start and end apart: 5, of which 3 were waited for; matrix products, arithmetic and copies ran while one was open for 0% of the time, Pallas kernels for 37%

profile of v2, /device:TPU:97, one launch (start us, length us, event | category | flops | bytes accessed | tf_op | source)
XLA Modules:
  0.0 66.2 jit_solution(15934261458084417637)
XLA Ops:
  0.0 0.1 pad_add_fusion.meta
  0.1 2.0 %pack.1.far_in = f32[128,8,128]{2,1,0:T(8,128)S(1)} custom-call(s32[2]{0:T(128)S(1)} %pad_add_fusion.meta, f32[128,32,128]{2,1,0:T(8,128)} %prev.5), custom_call_target="tpu_custom_call" | custom-call | flops 1000000000 | bytes 3000000 | tf_op jit(solution)/shard_map/pack/pallas_call | solution.py:387
  2.1 5.2 %collective-permute-start.1 = (f32[128,8,128]{2,1,0:T(8,128)S(1)}, f32[128,8,128]{2,1,0:T(8,128)S(1)}, u32[]{:S(2)}, u32[]{:S(2)}) collective-permute-start(f32[128,8,128]{2,1,0:T(8,128)S(1)} %pack.1.far_in), channel_id=1, source_target_pairs={{8,16},{16,8},{24,32},{32,24},{40,48},{48,40},{56,64},{64,56},{72,... | collective-permute-start | bytes 1572872 | tf_op jit(solution)/shard_map/ppermute | solution.py:415
  7.3 4.9 %spectrum.1 = (f32[128,8,128]{2,1,0:T(8,128)}, f32[8,4,128,128]{3,2,1,0:T(8,128)}) custom-call(s32[2]{0:T(128)S(1)} %pad_add_fusion.meta, f32[128,8,128]{2,1,0:T(8,128)S(1)} %pack.1.far_in, f32[128,32,128]{2,1,0:T(8,128)} %prev.5, f32[4096,128]{1,0:T(8,128)S(1)} %bitcast.3, f32[128,128]{1,0:T(8,128)S(1)} %copy-done.6, bf16[512,1024]{1,0:T(8,128)(2,1)S(1)} %copy-done.7, ...), custom_call_target="tpu_custom_call" | custom-call | flops 40000000000 | bytes 120000000 | tf_op jit(solution)/shard_map/spectrum/pallas_call | solution.py:387
  12.3 0.1 collective-permute-start
  12.4 0.0 copy-start.8
  12.4 0.0 copy-start
  12.4 0.0 copy-start.2
  12.4 0.0 copy-start.5
  12.4 4.4 %all-to-all-start = ((f32[8,4,128,128]{3,2,1,0:T(8,128)}), f32[8,4,128,128]{3,2,1,0:T(8,128)S(1)}, u32[]{:S(2)}, u32[]{:S(2)}) async-start(f32[8,4,128,128]{3,2,1,0:T(8,128)} %get-tuple-element.14), calls=%async_computation | async-start | bytes 4194304 | tf_op jit(solution)/shard_map/all_to_all | solution.py:467
  16.8 0.1 copy.16.near
  16.9 2.9 %collective-permute-done.1.far_in = f32[128,8,128]{2,1,0:T(8,128)S(1)} collective-permute-done((f32[128,8,128]{2,1,0:T(8,128)S(1)}, f32[128,8,128]{2,1,0:T(8,128)S(1)}, u32[]{:S(2)}, u32[]{:S(2)}) %collective-permute-start.1) | collective-permute-done | bytes 524320 | tf_op jit(solution)/shard_map/ppermute | solution.py:415
  19.8 0.0 copy-start.4
  19.8 1.6 %copy-done.4 = f32[128,32,128]{2,1,0:T(8,128)S(1)} copy-done((f32[128,32,128]{2,1,0:T(8,128)S(1)}, f32[128,32,128]{2,1,0:T(8,128)}, u32[]{:S(2)}) %copy-start.4) | copy-done | bytes 2097176
  21.4 8.0 %start.1 = (f32[32,128,128]{2,1,0:T(8,128)}, f32[8,128,128]{2,1,0:T(8,128)S(1)}) custom-call(s32[2]{0:T(128)S(1)} %pad_add_fusion.meta, s32[32,4]{1,0:T(8,128)S(1)} %copy.16.near, f32[32]{0:T(128)S(1)} %copy-done.1, f32[32]{0:T(128)S(1)} %copy-done.2, f32[128,32,128]{2,1,0:T(8,128)S(1)} %copy-done.4, f32[128,8,128]{2,1,0:T(8,128)} %collective-permute-done.near_in, ...), custom_call_target="tpu_custom_call" | custom-call | flops 60000002048 | bytes 180000000 | tf_op jit(solution)/shard_map/start/pallas_call | solution.py:387
  29.5 15.0 %all-to-all-done.rhs = f32[8,4,128,128]{3,2,1,0:T(8,128)S(1)} async-done(((f32[8,4,128,128]{3,2,1,0:T(8,128)}), f32[8,4,128,128]{3,2,1,0:T(8,128)S(1)}, u32[]{:S(2)}, u32[]{:S(2)}) %all-to-all-start) | async-done | bytes 2097184 | tf_op jit(solution)/shard_map/all_to_all | solution.py:467
  44.5 0.7 %far_edge.1.refs_0_ = f32[8,128,128]{2,1,0:T(8,128)S(1)} custom-call(s32[2]{0:T(128)S(1)} %pad_add_fusion.meta, f32[32]{0:T(128)S(1)} %copy-done.1, f32[32]{0:T(128)S(1)} %copy-done.2, f32[8,128,128]{2,1,0:T(8,128)S(1)} %get-tuple-element.16.base_in, f32[8,4,128,128]{3,2,1,0:T(8,128)S(1)} %all-to-all-done.rhs, f32[128,128]{1,0:T(8,128)S(1)} %copy-done), custom_call_target="tpu_custom_call" | custom-call | flops 1000000000 | bytes 3000000 | tf_op jit(solution)/shard_map/far_edge/pallas_call | solution.py:387
  45.2 6.3 %collective-permute-start.2 = (f32[8,128,128]{2,1,0:T(8,128)S(1)}, f32[8,128,128]{2,1,0:T(8,128)S(1)}, u32[]{:S(2)}, u32[]{:S(2)}) collective-permute-start(f32[8,128,128]{2,1,0:T(8,128)S(1)} %far_edge.1.refs_0_), channel_id=1, source_target_pairs={{8,16},{16,8},{24,32},{32,24},{40,48},{48,40},{56,64},{64,56},{72,... | collective-permute-start | bytes 1572872 | tf_op jit(solution)/shard_map/ppermute | solution.py:415
  51.5 1.7 %near_edge.1 = f32[8,128,128]{2,1,0:T(8,128)S(1)} custom-call(s32[2]{0:T(128)S(1)} %pad_add_fusion.meta, f32[32]{0:T(128)S(1)} %copy-done.1, f32[32]{0:T(128)S(1)} %copy-done.2, f32[32,128,128]{2,1,0:T(8,128)} %get-tuple-element.13.base_hbm.base_in, f32[8,4,128,128]{3,2,1,0:T(8,128)S(1)} %all-to-all-done.rhs, f32[128,128]{1,0:T(8,128)S(1)} %copy-done, ...), custom_call_target="tpu_custom_call" | custom-call | flops 1000000000 | bytes 3000000 | tf_op jit(solution)/shard_map/near_edge/pallas_call | solution.py:387
  53.3 0.3 collective-permute-start.3
  53.5 7.8 %second.1 = (f32[128,32,128]{2,1,0:T(8,128)}, f32[8,128,128]{2,1,0:T(8,128)S(1)}, f32[8,128,128]{2,1,0:T(8,128)S(1)}) custom-call(s32[2]{0:T(128)S(1)} %pad_add_fusion.meta, s32[32,4]{1,0:T(8,128)S(1)} %copy.16.near, f32[32]{0:T(128)S(1)} %copy-done.1, f32[32]{0:T(128)S(1)} %copy-done.2, f32[32,128,128]{2,1,0:T(8,128)} %get-tuple-element.13.base_hbm.base_in, ...), custom_call_target="tpu_custom_call" | custom-call | flops 15000000512 | bytes 45000000 | tf_op jit(solution)/shard_map/second/pallas_call | solution.py:387
  61.4 2.1 %near_finish.1.kept = f32[128,32,128]{2,1,0:T(8,128)} custom-call(s32[2]{0:T(128)S(1)} %pad_add_fusion.meta, s32[32,4]{1,0:T(8,128)S(1)} %copy.16.near, f32[32]{0:T(128)S(1)} %copy-done.1, f32[32]{0:T(128)S(1)} %copy-done.2, f32[8,128,128]{2,1,0:T(8,128)S(1)} %get-tuple-element.17.rest, ...), custom_call_target="tpu_custom_call", output_to_operand_aliasing={{}: (8, {})} | custom-call | flops 2000000000 | bytes 6000000 | tf_op jit(solution)/shard_map/near_finish/pallas_call | solution.py:387
  63.4 0.6 collective-permute-done.2.beside
  64.0 2.0 %far_finish.1 = f32[128,32,128]{2,1,0:T(8,128)} custom-call(s32[2]{0:T(128)S(1)} %pad_add_fusion.meta, s32[32,4]{1,0:T(8,128)S(1)} %copy.16.near, f32[32]{0:T(128)S(1)} %copy-done.1, f32[32]{0:T(128)S(1)} %copy-done.2, f32[8,128,128]{2,1,0:T(8,128)S(1)} %get-tuple-element.15.rest, ...), custom_call_target="tpu_custom_call", output_to_operand_aliasing={{}: (8, {})} | custom-call | flops 2000000000 | bytes 6000000 | tf_op jit(solution)/shard_map/far_finish/pallas_call | solution.py:387
  (14 shorter events, 0.0 us)
Async XLA Ops:
  0.0 7.3 %copy-start.6 = (f32[128,128]{1,0:T(8,128)S(1)}, f32[128,128]{1,0:T(8,128)}, u32[]{:S(2)}) copy-start(f32[128,128]{1,0:T(8,128)} %der.1) | copy-start | bytes 196612
  0.0 7.3 %copy-start.3 = (f32[1024,4,128]{2,1,0:T(4,128)S(1)}, f32[1024,4,128]{2,1,0:T(4,128)}, u32[]{:S(2)}) copy-start(f32[1024,4,128]{2,1,0:T(4,128)} %param.10) | copy-start | bytes 6291460
  0.0 7.3 %copy-start.7 = (bf16[512,1024]{1,0:T(8,128)(2,1)S(1)}, bf16[512,1024]{1,0:T(8,128)(2,1)}, u32[]{:S(2)}) copy-start(bf16[512,1024]{1,0:T(8,128)(2,1)} %constant.13.clone.odd_table) | copy-start | bytes 3145732
  2.1 17.7 %collective-permute-start.1 = (f32[128,8,128]{2,1,0:T(8,128)S(1)}, f32[128,8,128]{2,1,0:T(8,128)S(1)}, u32[]{:S(2)}, u32[]{:S(2)}) collective-permute-start(f32[128,8,128]{2,1,0:T(8,128)S(1)} %pack.1.far_in), channel_id=1, source_target_pairs={{8,16},{16,8},{24,32},{32,24},{40,48},{48,40},{56,64},{64,56},{72,... | collective-permute-start | bytes 1572872 | tf_op jit(solution)/shard_map/ppermute | solution.py:415
  12.3 7.5 %collective-permute-start = (f32[128,8,128]{2,1,0:T(8,128)}, f32[128,8,128]{2,1,0:T(8,128)}, u32[]{:S(2)}, u32[]{:S(2)}) collective-permute-start(f32[128,8,128]{2,1,0:T(8,128)} %get-tuple-element.12), channel_id=1, source_target_pairs={{0,8},{8,0},{16,24},{24,16},{32,40},{40,32},{48,56},{56,48},{64,72... | collective-permute-start | bytes 1572872 | tf_op jit(solution)/shard_map/ppermute | solution.py:415
  12.4 4.4 %copy-start.8 = (s32[32,4]{0,1:T(4,128)S(1)}, s32[32,4]{0,1:T(4,128)}, u32[]{:S(2)}) copy-start(s32[32,4]{0,1:T(4,128)} %param.17) | copy-start | bytes 1540
  12.4 7.4 %copy-start = (f32[128,128]{1,0:T(8,128)S(1)}, f32[128,128]{1,0:T(8,128)}, u32[]{:S(2)}) copy-start(f32[128,128]{1,0:T(8,128)} %stiff.11) | copy-start | bytes 196612
  12.4 7.4 %copy-start.1 = (f32[32]{0:T(128)S(1)}, f32[32]{0:T(128)}, u32[]{:S(2)}) copy-start(f32[32]{0:T(128)} %reaction.11) | copy-start | bytes 388
  12.4 7.4 %copy-start.2 = (f32[32]{0:T(128)S(1)}, f32[32]{0:T(128)}, u32[]{:S(2)}) copy-start(f32[32]{0:T(128)} %axial.11) | copy-start | bytes 388
  12.4 7.4 %copy-start.5 = (f32[4,128,128]{2,1,0:T(8,128)S(1)}, f32[4,128,128]{2,1,0:T(8,128)}, u32[]{:S(2)}) copy-start(f32[4,128,128]{2,1,0:T(8,128)} %coupling.7) | copy-start | bytes 786436
  12.4 32.1 %all-to-all-start = ((f32[8,4,128,128]{3,2,1,0:T(8,128)}), f32[8,4,128,128]{3,2,1,0:T(8,128)S(1)}, u32[]{:S(2)}, u32[]{:S(2)}) async-start(f32[8,4,128,128]{3,2,1,0:T(8,128)} %get-tuple-element.14), calls=%async_computation | async-start | bytes 4194304 | tf_op jit(solution)/shard_map/all_to_all | solution.py:467
  19.8 1.6 %copy-start.4 = (f32[128,32,128]{2,1,0:T(8,128)S(1)}, f32[128,32,128]{2,1,0:T(8,128)}, u32[]{:S(2)}) copy-start(f32[128,32,128]{2,1,0:T(8,128)} %prev.5) | copy-start | bytes 6291460
  45.2 18.8 %collective-permute-start.2 = (f32[8,128,128]{2,1,0:T(8,128)S(1)}, f32[8,128,128]{2,1,0:T(8,128)S(1)}, u32[]{:S(2)}, u32[]{:S(2)}) collective-permute-start(f32[8,128,128]{2,1,0:T(8,128)S(1)} %far_edge.1.refs_0_), channel_id=1, source_target_pairs={{8,16},{16,8},{24,32},{32,24},{40,48},{48,40},{56,64},{64,56},{72,... | collective-permute-start | bytes 1572872 | tf_op jit(solution)/shard_map/ppermute | solution.py:415
  53.3 8.1 %collective-permute-start.3 = (f32[8,128,128]{2,1,0:T(8,128)S(1)}, f32[8,128,128]{2,1,0:T(8,128)S(1)}, u32[]{:S(2)}, u32[]{:S(2)}) collective-permute-start(f32[8,128,128]{2,1,0:T(8,128)S(1)} %near_edge.1), channel_id=1, source_target_pairs={{0,8},{8,0},{16,24},{24,16},{32,40},{40,32},{48,56},{56,48},{64,72... | collective-permute-start | bytes 1572872 | tf_op jit(solution)/shard_map/ppermute | solution.py:415
